TPU v7x, 128 devices: a whole 4x4x4 slice. The times are simulated.
128 devices in a mesh: attn: 16 (over z, x), exp: 8 (over y, core).
Axes of the slice: x: 4, y: 4, z: 4, core: 2. Of those that a mesh axis runs over, the one named last changes fastest.
Arguments:
- hidden_in: bfloat16 [128, 4096], P(('attn', 'exp')), may hold values from -6 to 6
- query: bfloat16 [128, 4096], P(('attn', 'exp')), may hold values from -240 to 240, as said below
- key_latent: bfloat16 [128, 1024, 512], P(('attn', 'exp')), may hold values from -6 to 6
- value_latent: bfloat16 [128, 1024, 512], P(('attn', 'exp')), may hold values from -6 to 6
- lengths: int32 [128], P(('attn', 'exp')), may hold values from 128 to 1024, as said below
- key_up: bfloat16 [512, 1024], replicated, may hold values from -0.25 to 0.25
- value_up: bfloat16 [512, 1024], replicated, may hold values from -0.25 to 0.25
- norm_gain: bfloat16 [4096], replicated, may hold values from 0.5 to 2
- router_weight: bfloat16 [4096, 8], replicated, may hold values from -0.09375 to 0.09375
- route_ids: int32 [128, 2], replicated, may hold values from 0 to 7, all different within a row; in each aligned block of 128 rows (0 to 127, 128 to 255, ...) at most 64 rows name the same one
- gate_weight: bfloat16 [8, 4096, 14336], P('exp', None, 'attn'), may hold values from -0.09375 to 0.09375
- up_weight: bfloat16 [8, 4096, 14336], P('exp', None, 'attn'), may hold values from -0.09375 to 0.09375
- down_weight: bfloat16 [8, 14336, 4096], P('exp', 'attn'), may hold values from -0.046875 to 0.046875
Outputs:
- mixed: bfloat16 [128, 4096], P(('attn', 'exp'))
Inputs may be any that keep to these rules, and one draw needn't show every extreme that they name: `query`: query rows of order one; a row of a head may carry a common scale of up to some tens. `lengths`: in every draw one request has all 1024 slots live and one has 128. `route_ids`: A token's 2 experts differ; no expert is named by more than 64 tokens, a bound that some block reaches.
All inputs are finite; a program needn't handle non-finite values.
Results may differ from a plain program's by a relative error of at most 0.023.
Values may be sent and summed in bfloat16 or wider, within the bound.
No kernel may reach another device: no remote copies, remote signals or barrier semaphores. Data moves between devices by JAX's collectives and lax.ppermute only.
A program may use at most 128 MiB of HBM per device.

v0:
```python
import jax
import jax.numpy as jnp
from jax import lax
from jax.sharding import PartitionSpec as P

HEADS = 32
KV_HEADS = 8
HEAD_DIM = 128
EXPERTS = 8
TOP = 2


def masked_softmax(scores, lengths):
    slots = scores.shape[-1]
    usable = jnp.arange(slots, dtype=jnp.int32)[None, :] < lengths[:, None]
    usable = usable[:, None, None, :]
    scores = jnp.where(usable, scores, jnp.float32(-1e30))
    peak_score = jnp.max(scores, axis=-1, keepdims=True)
    weights = jnp.where(usable, jnp.exp(scores - peak_score), jnp.float32(0.0))
    return weights / jnp.sum(weights, axis=-1, keepdims=True)


def dense_gates(logits, chosen_ids):
    onehot_ids = (
        chosen_ids[:, :, None] == jnp.arange(EXPERTS, dtype=jnp.int32)[None, None, :]
    ).astype(jnp.float32)
    chosen_logits = jnp.einsum("te,tke->tk", logits, onehot_ids, precision=lax.Precision.HIGHEST)
    gates = jax.nn.softmax(chosen_logits, axis=1)
    return jnp.einsum("tk,tke->te", gates, onehot_ids, precision=lax.Precision.HIGHEST)


def body(
    hidden_in,
    query,
    key_latent,
    value_latent,
    lengths,
    key_up,
    value_up,
    norm_gain,
    router_weight,
    route_ids,
    gate_weight,
    up_weight,
    down_weight,
):
    requests, context, latent_rank = key_latent.shape
    width = hidden_in.shape[1]
    group = HEADS // KV_HEADS
    query_heads = query.reshape(requests, KV_HEADS, group, HEAD_DIM)
    rebuilt_keys = jnp.einsum(
        "rtc,ck->rtk", key_latent, key_up, preferred_element_type=jnp.float32
    ).reshape(requests, context, KV_HEADS, HEAD_DIM)
    rebuilt_values = jnp.einsum(
        "rtc,ck->rtk", value_latent, value_up, preferred_element_type=jnp.float32
    ).reshape(requests, context, KV_HEADS, HEAD_DIM)
    scores = jnp.einsum(
        "rkgd,rtkd->rkgt",
        query_heads.astype(jnp.float32),
        rebuilt_keys,
        precision=lax.Precision.HIGHEST,
    ) * HEAD_DIM ** (-0.5)
    weights = masked_softmax(scores, lengths)
    attended = jnp.einsum(
        "rkgt,rtkd->rkgd", weights, rebuilt_values, precision=lax.Precision.HIGHEST
    )
    attended = attended.reshape(requests, width)
    hidden = (hidden_in.astype(jnp.float32) + attended).astype(jnp.bfloat16)
    hidden_wide = hidden.astype(jnp.float32)
    scale_row = lax.rsqrt(jnp.mean(hidden_wide * hidden_wide, axis=-1, keepdims=True) + 1e-05)
    normed = (hidden_wide * scale_row * norm_gain.astype(jnp.float32)).astype(jnp.bfloat16)
    everyone = lax.all_gather(normed, ("attn", "exp"), axis=0, tiled=True)
    all_tokens = everyone.shape[0]
    attn_count = lax.axis_size("attn")
    experts_here = gate_weight.shape[0]
    first_expert = lax.axis_index("exp") * experts_here
    local_ids = first_expert + jnp.arange(experts_here, dtype=jnp.int32)
    routed = jnp.any(route_ids[:, :, None] == local_ids[None, None, :], axis=1)
    slot_index = jnp.cumsum(routed.astype(jnp.int32), axis=0) - 1
    capacity = 2 * all_tokens * TOP // EXPERTS
    placement = (
        slot_index.T[:, None, :] == jnp.arange(capacity, dtype=jnp.int32)[None, :, None]
    ) & routed.T[:, None, :]
    placement_bf = placement.astype(jnp.bfloat16)
    picked = jnp.einsum(
        "lct,td->lcd", placement_bf, everyone, preferred_element_type=jnp.float32
    ).astype(jnp.bfloat16)
    gate_part = jnp.einsum("lcd,ldf->lcf", picked, gate_weight, preferred_element_type=jnp.float32)
    up_part = jnp.einsum("lcd,ldf->lcf", picked, up_weight, preferred_element_type=jnp.float32)
    activation = (jax.nn.silu(gate_part) * up_part).astype(jnp.bfloat16)
    partial_out = jnp.einsum(
        "lcf,lfd->lcd", activation, down_weight, preferred_element_type=jnp.float32
    )
    token_share = all_tokens // attn_count
    placement_wide = placement.astype(jnp.float32)
    token_totals = lax.psum_scatter(
        jnp.einsum("lct,lcd->tld", placement_wide, partial_out, precision=lax.Precision.HIGHEST)
        .reshape(token_share * lax.axis_size("attn"), experts_here * width)
        .astype(jnp.bfloat16),
        "attn",
        scatter_dimension=0,
        tiled=True,
    )
    expert_out = token_totals.reshape(token_share, experts_here, width)
    block_start = lax.axis_index("attn") * token_share
    block_rows = lax.dynamic_slice_in_dim(everyone, block_start, token_share, 0)
    block_ids = lax.dynamic_slice_in_dim(route_ids, block_start, token_share, 0)
    block_logits = jnp.dot(block_rows, router_weight, preferred_element_type=jnp.float32)
    block_gates = lax.dynamic_slice_in_dim(
        dense_gates(block_logits, block_ids), first_expert, experts_here, 1
    )
    weighted = jnp.einsum(
        "tl,tld->td", block_gates, expert_out.astype(jnp.float32), precision=lax.Precision.HIGHEST
    )
    combined = lax.psum_scatter(
        weighted.astype(jnp.bfloat16), "exp", scatter_dimension=0, tiled=True
    ).astype(jnp.float32)
    return (hidden_wide + combined).astype(jnp.bfloat16)


def solution(mesh):
    in_specs = (
        P(("attn", "exp"), None),
        P(("attn", "exp"), None),
        P(("attn", "exp"), None, None),
        P(("attn", "exp"), None, None),
        P(("attn", "exp")),
        P(),
        P(),
        P(),
        P(),
        P(),
        P("exp", None, "attn"),
        P("exp", None, "attn"),
        P("exp", "attn", None),
    )
    out_specs = P(("attn", "exp"), None)
    return jax.shard_map(body, mesh=mesh, in_specs=in_specs, out_specs=out_specs, check_vma=False)
```

profile of v0, /device:TPU:0, one launch (start us, length us, event | category | flops | bytes accessed | tf_op | source)
XLA Modules:
  0.0 269.4 jit_solution(4881205945566844293)
XLA Ops:
  6.5 0.0 copy-start
  6.5 0.0 all-gather.3.cloned.1.call-start
  7.3 0.0 copy-start.4
  7.3 1.5 copy.51
  8.8 0.0 copy-done
  8.8 0.0 copy-start.1
  8.8 3.2 %fusion.23 = f32[1024,8,128]{2,0,1:T(8,128)} fusion(bf16[8,128,512]{2,1,0:T(8,128)(2,1)S(1)} %bitcast.80, bf16[1,1024,512]{2,1,0:T(8,128)(2,1)S(1)} %copy-done), kind=kOutput, calls=%fused_computation.22 | convolution fusion | flops 1073741824 | bytes 6291456 | tf_op jit(solution)/shard_map/rtc,ck->rtk/dot_general | solution.py:51
  12.0 0.0 copy-done.4
  12.0 0.1 reduce.8
  12.1 4.1 %fusion.18 = f32[8,4,1024]{2,1,0:T(4,128)S(1)} fusion(f32[1024,8,128]{2,0,1:T(8,128)} %fusion.23, bf16[8,4,128]{2,1,0:T(4,128)(2,1)S(1)} %bitcast.88, pred[1024]{0:T(1024)(128)(4,1)S(1)} %iota_compare_fusion.3), kind=kOutput, calls=%fused_computation.17 | convolution fusion | flops 50397184 | bytes 4334592 | tf_op jit(solution)/shard_map/rkgd,rtkd->rkgt/dot_general | solution.py:57
  16.2 0.2 fusion.50
  16.5 0.0 copy-done.1
  16.5 0.5 copy.52
  17.0 0.0 copy-start.2
  17.0 0.0 copy-start.5
  17.0 0.0 copy-start.6
  17.1 0.0 copy-start.8
  17.1 2.5 fusion.21
  19.6 2.1 fusion.32
  21.7 0.0 copy-done.2
  21.7 0.6 multiply_reduce_fusion
  23.1 0.0 copy-done.5
  23.1 0.6 convert_bitcast_fusion
  23.7 0.0 all-gather.3.cloned.1.call-update
  23.8 0.2 all-reduce.5.cloned.1.call-start
  24.0 0.0 copy-done.6
  24.0 0.1 constant_dynamic-slice_fusion.3
  24.1 0.1 copy.40
  24.2 0.1 copy.41
  24.3 0.2 reduce-window.7
  24.5 0.0 copy-done.8
  24.5 0.6 dynamic-slice.1
  25.7 0.1 add_reduce_fusion
  25.8 65.9 %all-gather.3.cloned.1.call-done = bf16[128,1,4096]{2,1,0:T(2,128)(2,1)} async-done(((bf16[1,1,4096]{2,1,0:T(2,128)(2,1)}), bf16[128,1,4096]{2,1,0:T(2,128)(2,1)}) %all-gather.3.cloned.1.call-update) | async-done | bytes 1048592 | tf_op jit(solution)/shard_map/all_gather | solution.py:72
  91.7 2.9 %convolution_convert_fusion.1 = bf16[64,4096]{1,0:T(8,128)(2,1)S(1)} fusion(bf16[128,1,4096]{2,1,0:T(2,128)(2,1)} %all-gather.3.cloned.1.call-done, s32[128]{0:T(128)S(1)} %add_reduce_fusion, pred[128]{0:T(512)(128)(4,1)S(1)} %compare_reduce_fusion), kind=kOutput, calls=%fused_computation.9 | convolution fusion | flops 67387392 | bytes 1573504 | tf_op jit(solution)/shard_map/lct,td->lcd/dot_general | solution.py:85
  94.6 4.3 %fusion.5 = f32[64,896]{1,0:T(8,128)S(1)} fusion(bf16[64,4096]{1,0:T(8,128)(2,1)S(1)} %convolution_convert_fusion.1, bf16[1,4096,896]{2,1,0:T(8,128)(2,1)} %param.23), kind=kOutput, calls=%fused_computation.5 | convolution fusion | flops 469762048 | bytes 8093696 | tf_op jit(solution)/shard_map/lcd,ldf->lcf/dot_general | solution.py:88
  98.9 0.0 copy-start.3
  98.9 7.9 %fusion.1 = f32[64,4096]{1,0:T(8,128)S(1)} fusion(bf16[1,896,4096]{2,1,0:T(8,128)(2,1)} %param.25, bf16[64,4096]{1,0:T(8,128)(2,1)S(1)} %convolution_convert_fusion.1, bf16[1,4096,896]{2,1,0:T(8,128)(2,1)} %param.24, f32[64,896]{1,0:T(8,128)S(1)} %fusion.5), kind=kOutput, calls=%fused_computation.1 | convolution fusion | flops 939868160 | bytes 16482304 | tf_op jit(solution)/shard_map/lcf,lfd->lcd/dot_general | solution.py:91
  106.9 0.0 copy-start.7
  106.9 2.8 %fusion.7 = bf16[128,4096]{0,1:T(8,128)(2,1)} fusion(f32[64,4096]{1,0:T(8,128)S(1)} %fusion.1, s32[128]{0:T(128)S(1)} %add_reduce_fusion, pred[128]{0:T(512)(128)(4,1)S(1)} %compare_reduce_fusion), kind=kOutput, calls=%fused_computation.8 | convolution fusion | flops 403193856 | bytes 2097792 | tf_op jit(solution)/shard_map/lct,lcd->tld/dot_general | solution.py:97
  109.7 0.0 all-reduce.5.cloned.1.call-update
  109.7 0.0 all-reduce.7.cloned.1.call-start
  109.7 1.0 constant_dynamic-slice_fusion.4
  110.8 0.0 copy-done.3
  110.8 0.2 fusion.35
  111.0 0.2 fusion.44
  111.2 0.1 copy.46
  111.4 0.1 copy.60
  111.4 0.1 select_reduce_fusion
  111.6 0.1 constant_dynamic-slice_fusion.2
  111.6 0.1 copy.59
  111.7 82.7 %all-reduce.5.cloned.1.call-done = bf16[128,4096]{0,1:T(8,128)(2,1)} async-done(((bf16[128,4096]{0,1:T(8,128)(2,1)}), bf16[128,4096]{0,1:T(8,128)(2,1)}) %all-reduce.5.cloned.1.call-update) | async-done | bytes 1048592
  194.5 1.6 constant_dynamic-slice_fusion.1
  196.0 0.3 copy.42
  196.3 0.1 multiply_convert_fusion
  196.4 1.4 copy.43
  197.8 0.0 all-reduce.7.cloned.1.call-update
  197.8 0.0 copy-done.7
  197.8 0.6 dynamic-slice.3
  198.4 61.2 %all-reduce.7.cloned.1.call-done = bf16[8,4096]{0,1:T(8,128)(2,1)} async-done(((bf16[8,4096]{0,1:T(8,128)(2,1)}), bf16[8,4096]{0,1:T(8,128)(2,1)}) %all-reduce.7.cloned.1.call-update) | async-done | bytes 65552
  259.6 2.2 constant_dynamic-slice_fusion
  261.8 0.4 copy.44
  262.2 0.7 add_convert_fusion
  (7 shorter events, 0.1 us)
Async XLA Ops:
  6.5 2.3 copy-start
  6.5 85.2 %all-gather.3.cloned.1.call-start = ((), (), s32[]{:S(2)}) async-start(), calls=%async_computation | async-start | bytes 2113536 | tf_op jit(solution)/shard_map/all_gather | solution.py:72
  7.3 4.8 %copy-start.4 = (bf16[1,4096]{1,0:T(2,128)(2,1)S(1)}, bf16[1,4096]{1,0:T(2,128)(2,1)}, u32[]{:S(2)}) copy-start(bf16[1,4096]{1,0:T(2,128)(2,1)} %param.14) | copy-start | bytes 24580
  8.8 7.6 %copy-start.1 = (bf16[512,1024]{1,0:T(8,128)(2,1)S(1)}, bf16[512,1024]{1,0:T(8,128)(2,1)}, u32[]{:S(2)}) copy-start(bf16[512,1024]{1,0:T(8,128)(2,1)} %param.19) | copy-start | bytes 3145732
  17.0 4.7 %copy-start.2 = (bf16[1,4096]{1,0:T(2,128)(2,1)S(1)}, bf16[1,4096]{1,0:T(2,128)(2,1)}, u32[]{:S(2)}) copy-start(bf16[1,4096]{1,0:T(2,128)(2,1)} %param.13) | copy-start | bytes 24580
  17.0 6.0 %copy-start.5 = (bf16[4096]{0:T(1024)(128)(2,1)S(1)}, bf16[4096]{0:T(1024)(128)(2,1)}, u32[]{:S(2)}) copy-start(bf16[4096]{0:T(1024)(128)(2,1)} %param.20) | copy-start | bytes 24580
  17.0 7.0 %copy-start.6 = (s32[128,2]{0,1:T(2,128)S(1)}, s32[128,2]{0,1:T(2,128)}, u32[]{:S(2)}) copy-start(s32[128,2]{0,1:T(2,128)} %param.22) | copy-start | bytes 3076
  17.1 7.4 %copy-start.8 = (u32[128]{0:T(128)S(1)}, u32[128]{0:T(128)}, u32[]{:S(2)}) copy-start(u32[128]{0:T(128)} %constant.55) | copy-start | bytes 1540
  23.8 170.7 %all-reduce.5.cloned.1.call-start = ((), (), s32[]{:S(2)}) async-start(), calls=%async_computation.1 | async-start | bytes 2097152
  98.9 11.9 %copy-start.3 = (bf16[4096,8]{0,1:T(8,128)(2,1)S(1)}, bf16[4096,8]{0,1:T(8,128)(2,1)}, u32[]{:S(2)}) copy-start(bf16[4096,8]{0,1:T(8,128)(2,1)} %param.21) | copy-start | bytes 196612
  106.9 91.0 %copy-start.7 = (u32[128]{0:T(128)S(1)}, u32[128]{0:T(128)}, u32[]{:S(2)}) copy-start(u32[128]{0:T(128)} %constant.59) | copy-start | bytes 1540
  109.7 149.9 %all-reduce.7.cloned.1.call-start = ((), (), s32[]{:S(2)}) async-start(), calls=%async_computation.2 | async-start | bytes 2097152
Sparse Core Ops, SparseCore 0:
  23.9 67.7 all-gather.2
  109.8 84.5 all-reduce.4
  198.0 61.6 all-reduce.6
where the time goes:
time: 270 us; the launch traced here: 269 us
  waiting for transfers between devices  210 us (78%)
  matrix products  30.3 us (11%)
  between operations  15.4 us (6%)
  local copies, waits for them, and re-layouts  10.8 us (4%)
  other arithmetic  2.76 us (1%)
    unnamed x5, waiting for transfers between devices  144 us
    all_gather x1, waiting for transfers between devices, body(): everyone = lax.all_gather(normed, ('attn', 'exp'), axis=0, tiled=True)  65.9 us
    dot_general x1, matrix products, body(): jnp.einsum('lcf,lfd->lcd', activation, down_weight, preferred_element_typ...  7.92 us
  transfers between devices with their start and end apart: 3, of which 3 were waited for; matrix products, arithmetic and copies ran while one was open for 1% of the time, Pallas kernels for 0%

commit v1 on v0

v1 whole, which is shorter than its diff:
```python
import jax
import jax.numpy as jnp
from jax import lax
from jax.experimental import pallas as pl
from jax.experimental.pallas import tpu as pltpu
from jax.sharding import Mesh, PartitionSpec as P

KV_HEADS = 8
GROUP = 4
HEAD_DIM = 128
RANK = 512
CTX = 1024
D = 4096
ROWS = 8
COLS = 512
CHIPS = 64
CHIP_AXES = ("z", "x", "y")
ALL_AXES = ("z", "x", "y", "core")
F32 = jnp.float32
BF16 = jnp.bfloat16
VMEM = pl.BlockSpec(memory_space=pltpu.VMEM)
SMEM = pl.BlockSpec(memory_space=pltpu.SMEM)


def parts_of(x, n):
    out = []
    for _ in range(n):
        p = x.astype(BF16)
        out.append(p)
        x = x - p.astype(F32)
    return out


def dot_nt(a, b):
    return lax.dot_general(a, b, (((1,), (1,)), ((), ())), preferred_element_type=F32)


def to_rows(ref, scratch):
    for s in range(ROWS):
        scratch[s : s + 1, :] = ref[0:1, s * COLS : (s + 1) * COLS].astype(F32)
    return scratch[...]


def attend_kernel(
    length, query, hidden_in, gain, key_latent, value_latent, key_up, value_up,
    sent, hidden_out, rows_scratch,
):
    q = to_rows(query, rows_scratch)
    kv_row = lax.broadcasted_iota(jnp.int32, (KV_HEADS, KV_HEADS * HEAD_DIM), 0)
    kv_col = lax.broadcasted_iota(jnp.int32, (KV_HEADS, KV_HEADS * HEAD_DIM), 1) // HEAD_DIM
    own_block = kv_row == kv_col
    spread = []
    for g in range(GROUP):
        piece = q[:, g * HEAD_DIM : (g + 1) * HEAD_DIM]
        spread.append(jnp.where(own_block, jnp.concatenate([piece] * KV_HEADS, axis=1), 0.0))
    spread = jnp.concatenate(spread, axis=0).astype(BF16)
    folded = dot_nt(spread, key_up[...])
    heads = KV_HEADS * GROUP
    stacked = jnp.concatenate(parts_of(folded, 3), axis=0)
    s3 = dot_nt(stacked, key_latent[0])
    scores = (s3[:heads] + s3[heads : 2 * heads] + s3[2 * heads :]) * HEAD_DIM ** (-0.5)
    usable = lax.broadcasted_iota(jnp.int32, (heads, CTX), 1) < length[0]
    scores = jnp.where(usable, scores, -1e30)
    peak = jnp.max(scores, axis=1, keepdims=True)
    weights = jnp.where(usable, jnp.exp(scores - peak), 0.0)
    total = jnp.sum(weights, axis=1, keepdims=True)
    w2 = jnp.concatenate(parts_of(weights, 2), axis=0)
    l2 = jnp.dot(w2, value_latent[0], preferred_element_type=F32)
    latent = (l2[:heads] + l2[heads:]) / total
    v2 = jnp.dot(jnp.concatenate(parts_of(latent, 2), axis=0), value_up[...], preferred_element_type=F32)
    values = v2[:heads] + v2[heads:]
    attended = []
    for g in range(GROUP):
        mine = jnp.where(own_block, values[g * KV_HEADS : (g + 1) * KV_HEADS], 0.0)
        acc = mine[:, :HEAD_DIM]
        for k in range(1, KV_HEADS):
            acc = acc + mine[:, k * HEAD_DIM : (k + 1) * HEAD_DIM]
        attended.append(acc)
    attended = jnp.concatenate(attended, axis=1)
    hidden = (to_rows(hidden_in, rows_scratch) + attended).astype(BF16).astype(F32)
    hidden_out[...] = hidden
    square = jnp.sum(jnp.sum(hidden * hidden, axis=1, keepdims=True), axis=0, keepdims=True)
    scale = lax.rsqrt(square * (1.0 / D) + 1e-05)
    normed = (hidden * scale * to_rows(gain, rows_scratch)).astype(BF16)
    sent[...] = jnp.broadcast_to(normed[None], sent.shape)


def expert_kernel(
    expert, own, other, ids, router, gate, up, down,
    out_own, out_other, wide, rows,
):
    half = CHIPS
    for i, block in enumerate((own, other)):
        wide[...] = block[...].astype(F32)
        for s in range(ROWS):
            rows[i * half : (i + 1) * half, s * COLS : (s + 1) * COLS] = wide[:, s, :].astype(BF16)
    x = rows[...]
    g = jnp.dot(x, gate[0], preferred_element_type=F32)
    u = jnp.dot(x, up[0], preferred_element_type=F32)
    act = (g * jax.nn.sigmoid(g) * u).astype(BF16)
    logits = jnp.dot(x, router[...], preferred_element_type=F32)
    lane = lax.broadcasted_iota(jnp.int32, logits.shape, 1)
    first, second = ids[:, 0:1], ids[:, 1:2]
    logit_a = jnp.sum(jnp.where(lane == first, logits, 0.0), axis=1, keepdims=True)
    logit_b = jnp.sum(jnp.where(lane == second, logits, 0.0), axis=1, keepdims=True)
    peak = jnp.maximum(logit_a, logit_b)
    exp_a, exp_b = jnp.exp(logit_a - peak), jnp.exp(logit_b - peak)
    mine = jnp.where(first == expert[0], exp_a, 0.0) + jnp.where(second == expert[0], exp_b, 0.0)
    weight = mine / (exp_a + exp_b)
    for i, out in enumerate((out_own, out_other)):
        for s in range(ROWS):
            part = jnp.dot(
                act[i * half : (i + 1) * half],
                down[0, :, s * COLS : (s + 1) * COLS],
                preferred_element_type=F32,
            )
            wide[:, s, :] = part * weight[i * half : (i + 1) * half]
        out[...] = wide[...].astype(BF16)


def add_kernel(a, b, out):
    out[...] = (a[...].astype(F32) + b[...].astype(F32)).astype(BF16)


def finish_kernel(parts, hidden, out):
    total = jnp.sum(parts[...].astype(F32), axis=0) + hidden[...]
    for s in range(ROWS):
        out[0:1, s * COLS : (s + 1) * COLS] = total[s : s + 1, :].astype(BF16)


def swap_cores(x):
    return lax.ppermute(x, "core", [(0, 1), (1, 0)])


def body(
    hidden_in, query, key_latent, value_latent, lengths, key_up, value_up,
    norm_gain, router_weight, route_ids, gate_weight, up_weight, down_weight,
):
    core = lax.axis_index("core")
    expert = lax.axis_index("y") * 2 + core
    token = jax.ShapeDtypeStruct((CHIPS, ROWS, COLS), BF16)
    sent, hidden = pl.pallas_call(
        attend_kernel,
        out_shape=(token, jax.ShapeDtypeStruct((ROWS, COLS), F32)),
        in_specs=[SMEM] + [VMEM] * 7,
        out_specs=(VMEM, VMEM),
        scratch_shapes=[pltpu.VMEM((ROWS, COLS), F32)],
        compiler_params=pltpu.CompilerParams(vmem_limit_bytes=24 * 2**20),
        name="attend",
    )(lengths, query, hidden_in, norm_gain.reshape(1, D), key_latent, value_latent, key_up, value_up)
    own = lax.all_to_all(sent, CHIP_AXES, 0, 0, tiled=True)
    other = swap_cores(own)
    by_chip = route_ids.reshape(CHIPS, 2, 2)
    ids = jnp.where(
        core == 0,
        jnp.concatenate([by_chip[:, 0], by_chip[:, 1]], axis=0),
        jnp.concatenate([by_chip[:, 1], by_chip[:, 0]], axis=0),
    )
    out_own, out_other = pl.pallas_call(
        expert_kernel,
        out_shape=(token, token),
        in_specs=[SMEM] + [VMEM] * 7,
        out_specs=(VMEM, VMEM),
        scratch_shapes=[
            pltpu.VMEM((CHIPS, ROWS, COLS), F32),
            pltpu.VMEM((2 * CHIPS, D), BF16),
        ],
        compiler_params=pltpu.CompilerParams(vmem_limit_bytes=48 * 2**20),
        name="experts",
    )(expert.reshape(1), own, other, ids, router_weight, gate_weight, up_weight, down_weight)
    summed = pl.pallas_call(
        add_kernel,
        out_shape=token,
        in_specs=[VMEM, VMEM],
        out_specs=VMEM,
        name="add_cores",
    )(out_own, swap_cores(out_other))
    parts = lax.all_to_all(summed, CHIP_AXES, 0, 0, tiled=True)
    return pl.pallas_call(
        finish_kernel,
        out_shape=jax.ShapeDtypeStruct((1, D), BF16),
        in_specs=[VMEM, VMEM],
        out_specs=VMEM,
        name="finish",
    )(parts, hidden)


def solution(mesh):
    fine = Mesh(mesh.devices.reshape(4, 4, 4, 2), ALL_AXES)
    in_specs = (
        P(ALL_AXES, None),
        P(ALL_AXES, None),
        P(ALL_AXES, None, None),
        P(ALL_AXES, None, None),
        P(ALL_AXES),
        P(),
        P(),
        P(),
        P(),
        P(),
        P(("y", "core"), None, ("z", "x")),
        P(("y", "core"), None, ("z", "x")),
        P(("y", "core"), ("z", "x"), None),
    )
    return jax.shard_map(
        body, mesh=fine, in_specs=in_specs, out_specs=P(ALL_AXES, None), check_vma=False
    )
```

time: 270 us -> 79.3 us (0.29)
  waiting for transfers between devices: 210 us -> 1.54 us
  blocking collectives: 0 us -> 44 us
  matrix products: 30.3 us -> 0 us
  Pallas kernels: 0 us -> 20.3 us
  between operations: 15.4 us -> 0.74 us
    unnamed x5 -> x0, waiting for transfers between devices: 144 us -> none
    all_gather x1 -> x0, waiting for transfers between devices: 65.9 us -> none  [body(): everyone = lax.all_gather(normed, ('attn', 'exp'), axis=0, tiled=True)]
    all_to_all x0 -> x2, blocking collectives: none -> 44 us  [the longest x1 24.6 us: body(): own = lax.all_to_all(sent, CHIP_AXES, 0, 0, tiled=True)]
    dot_general x10 -> x0, matrix products: 30.3 us -> none  [the longest x1 7.92 us: body(): jnp.einsum('lcf,lfd->lcd', activation, down_weight, preferred_element_typ...]
    pallas_call x0 -> x4, Pallas kernels: none -> 20.3 us  [the longest x1 14.9 us: body(): pl.pallas_call(expert_kernel, out_shape=(token, token), in_specs=[SMEM] +...]
    unnamed x24 -> x19, local copies, waits for them, and re-layouts: 5.21 us -> 9.24 us
  transfers between devices with their start and end apart: 3 -> 2, of which waited for: 3 -> 1; matrix products, arithmetic and copies ran while one was open for 1% -> 3% of each run, Pallas kernels for 0% -> 0%
where the time goes in v1:
time: 79.3 us; the launch traced here: 78.4 us
  blocking collectives  44 us (55%)
  Pallas kernels  20.3 us (26%)
  local copies, waits for them, and re-layouts  11.2 us (14%)
  waiting for transfers between devices  1.54 us (2%)
    all_to_all x1, blocking collectives, body(): own = lax.all_to_all(sent, CHIP_AXES, 0, 0, tiled=True)  24.6 us
    all_to_all x1, blocking collectives, body(): parts = lax.all_to_all(summed, CHIP_AXES, 0, 0, tiled=True)  19.5 us
    pallas_call x1, Pallas kernels, body(): pl.pallas_call(expert_kernel, out_shape=(token, token), in_specs=[SMEM] +...  14.9 us
    unnamed x19, local copies, waits for them, and re-layouts  9.24 us
    pallas_call x1, Pallas kernels, body(): pl.pallas_call(add_kernel, out_shape=token, in_specs=[VMEM, VMEM], out_sp...  2.12 us
    pallas_call x1, Pallas kernels, body(): pl.pallas_call(finish_kernel, out_shape=jax.ShapeDtypeStruct((1, D), BF16...  1.73 us
  transfers between devices with their start and end apart: 2, of which 1 were waited for; matrix products, arithmetic and copies ran while one was open for 3% of the time, Pallas kernels for 0%

profile of v1, /device:TPU:0, one launch (start us, length us, event | category | flops | bytes accessed | tf_op | source)
XLA Modules:
  0.0 78.4 jit_solution(12725487930579673341)
XLA Ops:
  0.7 0.7 reshape.10.gain
  1.4 0.0 copy-start
  1.4 1.2 %copy-done = bf16[1,1024,512]{2,1,0:T(8,128)(2,1)S(1)} copy-done((bf16[1,1024,512]{2,1,0:T(8,128)(2,1)S(1)}, bf16[1,1024,512]{2,1,0:T(8,128)(2,1)}, u32[]{:S(2)}) %copy-start) | copy-done | bytes 1048600
  2.6 0.0 copy-start.1
  2.6 1.2 %copy-done.1 = bf16[1,1024,512]{2,1,0:T(8,128)(2,1)S(1)} copy-done((bf16[1,1024,512]{2,1,0:T(8,128)(2,1)S(1)}, bf16[1,1024,512]{2,1,0:T(8,128)(2,1)}, u32[]{:S(2)}) %copy-start.1) | copy-done | bytes 1048600
  3.8 0.0 copy-start.2
  3.8 1.2 %copy-done.2 = bf16[512,1024]{1,0:T(8,128)(2,1)S(1)} copy-done((bf16[512,1024]{1,0:T(8,128)(2,1)S(1)}, bf16[512,1024]{1,0:T(8,128)(2,1)}, u32[]{:S(2)}) %copy-start.2) | copy-done | bytes 1048600
  5.0 0.0 copy-start.3
  5.0 1.2 %copy-done.3 = bf16[512,1024]{1,0:T(8,128)(2,1)S(1)} copy-done((bf16[512,1024]{1,0:T(8,128)(2,1)S(1)}, bf16[512,1024]{1,0:T(8,128)(2,1)}, u32[]{:S(2)}) %copy-start.3) | copy-done | bytes 1048600
  6.3 0.0 copy-start.5
  6.3 0.7 copy-done.5
  7.0 0.0 copy-start.6
  7.0 0.7 copy-done.6
  7.7 1.6 %attend.1 = (bf16[64,8,512]{2,1,0:T(8,128)(2,1)S(1)}, f32[8,512]{1,0:T(8,128)S(1)}) custom-call(s32[1]{0:T(128)S(6)} %copy.34.length, bf16[1,4096]{1,0:T(2,128)(2,1)S(1)} %copy-done.5, bf16[1,4096]{1,0:T(2,128)(2,1)S(1)} %copy-done.6, bf16[1,4096]{1,0:T(2,128)(2,1)S(1)} %reshape.10.gain, bf16[1,1024,512]{2,1,0:T(8,128)(2,1)S(1)} %copy-done, ...), custom_call_target="tpu_custom_call" | custom-call | tf_op jit(solution)/shard_map/attend/pallas_call | solution.py:142
  9.3 0.0 copy-start.7
  9.3 24.6 %all_to_all.10.own = bf16[64,8,512]{2,1,0:T(8,128)(2,1)S(1)} all-to-all(bf16[64,8,512]{2,1,0:T(8,128)(2,1)S(1)} %get-tuple-element.9), channel_id=1, replica_groups=mesh['z'=4,'x'=4,'y'=4,'core'=2] {'z','x','y'}, dimensions={0} | all-to-all | bytes 1048576 | tf_op jit(solution)/shard_map/all_to_all | solution.py:151
  33.8 0.0 copy-done.7
  33.8 0.0 collective-permute-start
  33.9 0.8 %reshape.11 = s32[64,2,2]{1,0,2:T(8,128)S(1)} reshape(s32[128,2]{0,1:T(2,128)} %param.22) | data formatting | bytes 2048 | tf_op jit(solution)/shard_map/reshape | solution.py:153
  34.7 0.2 slice_reduce_fusion.1
  34.9 0.1 pad_add_fusion.1
  34.9 0.1 copy.32
  35.0 0.1 copy.31
  35.2 1.3 %copy.33.router = bf16[4096,8]{1,0:T(8,128)(2,1)S(1)} copy(bf16[4096,8]{0,1:T(8,128)(2,1)} %param.21) | data formatting | bytes 131072 | tf_op args[8]
  36.5 0.0 collective-permute-done.other
  36.5 14.9 %experts.1 = (bf16[64,8,512]{2,1,0:T(8,128)(2,1)S(1)}, bf16[64,8,512]{2,1,0:T(8,128)(2,1)S(1)}) custom-call(s32[1]{0:T(128)} %bitcast.expert, bf16[64,8,512]{2,1,0:T(8,128)(2,1)S(1)} %all_to_all.10.own, bf16[64,8,512]{2,1,0:T(8,128)(2,1)S(1)} %collective-permute-done.other, s32[128,2]{1,0:T(8,128)S(1)} %broadcast_select_fusion.ids, ...), custom_call_target="tpu_custom_call" | custom-call | tf_op jit(solution)/shard_map/experts/pallas_call | solution.py:159
  51.4 0.0 copy-start.4
  51.4 0.8 copy-done.4
  52.2 0.5 collective-permute-start.1
  52.7 1.5 %collective-permute-done.1.b = bf16[64,8,512]{2,1,0:T(8,128)(2,1)S(1)} collective-permute-done((bf16[64,8,512]{2,1,0:T(8,128)(2,1)S(1)}, bf16[64,8,512]{2,1,0:T(8,128)(2,1)S(1)}, u32[]{:S(2)}, u32[]{:S(2)}) %collective-permute-start.1) | collective-permute-done | bytes 524320 | tf_op jit(solution)/shard_map/ppermute | solution.py:132
  54.2 0.0 copy-start.8
  54.2 0.8 %copy-done.8 = bf16[64,8,512]{2,1,0:T(8,128)(2,1)} copy-done((bf16[64,8,512]{2,1,0:T(8,128)(2,1)}, bf16[64,8,512]{2,1,0:T(8,128)(2,1)S(1)}, u32[]{:S(2)}) %copy-start.8) | copy-done | bytes 524312
  55.0 2.1 %add_cores.1 = bf16[64,8,512]{2,1,0:T(8,128)(2,1)} custom-call(bf16[64,8,512]{2,1,0:T(8,128)(2,1)} %copy-done.4, bf16[64,8,512]{2,1,0:T(8,128)(2,1)} %copy-done.8), custom_call_target="tpu_custom_call" | custom-call | tf_op jit(solution)/shard_map/add_cores/pallas_call | solution.py:171
  57.2 19.5 %all_to_all.11.parts = bf16[64,8,512]{2,1,0:T(8,128)(2,1)} all-to-all(bf16[64,8,512]{2,1,0:T(8,128)(2,1)} %add_cores.1), channel_id=1, replica_groups=mesh['z'=4,'x'=4,'y'=4,'core'=2] {'z','x','y'}, dimensions={0} | all-to-all | bytes 1048576 | tf_op jit(solution)/shard_map/all_to_all | solution.py:178
  76.6 1.7 %finish.1 = bf16[1,4096]{1,0:T(2,128)(2,1)} custom-call(bf16[64,8,512]{2,1,0:T(8,128)(2,1)} %all_to_all.11.parts, f32[8,512]{1,0:T(8,128)} %copy-done.7), custom_call_target="tpu_custom_call" | custom-call | tf_op jit(solution)/shard_map/finish/pallas_call | solution.py:179
  (1 shorter events, 0.0 us)
Async XLA Ops:
  1.4 1.2 %copy-start = (bf16[1,1024,512]{2,1,0:T(8,128)(2,1)S(1)}, bf16[1,1024,512]{2,1,0:T(8,128)(2,1)}, u32[]{:S(2)}) copy-start(bf16[1,1024,512]{2,1,0:T(8,128)(2,1)} %key_latent.1) | copy-start | bytes 3145732
  2.6 1.2 %copy-start.1 = (bf16[1,1024,512]{2,1,0:T(8,128)(2,1)S(1)}, bf16[1,1024,512]{2,1,0:T(8,128)(2,1)}, u32[]{:S(2)}) copy-start(bf16[1,1024,512]{2,1,0:T(8,128)(2,1)} %value_latent.1) | copy-start | bytes 3145732
  3.8 1.2 %copy-start.2 = (bf16[512,1024]{1,0:T(8,128)(2,1)S(1)}, bf16[512,1024]{1,0:T(8,128)(2,1)}, u32[]{:S(2)}) copy-start(bf16[512,1024]{1,0:T(8,128)(2,1)} %key_up.1) | copy-start | bytes 3145732
  5.0 1.2 %copy-start.3 = (bf16[512,1024]{1,0:T(8,128)(2,1)S(1)}, bf16[512,1024]{1,0:T(8,128)(2,1)}, u32[]{:S(2)}) copy-start(bf16[512,1024]{1,0:T(8,128)(2,1)} %value_up.1) | copy-start | bytes 3145732
  6.3 0.7 copy-start.5
  7.0 0.7 copy-start.6
  9.3 24.6 %copy-start.7 = (f32[8,512]{1,0:T(8,128)}, f32[8,512]{1,0:T(8,128)S(1)}, u32[]{:S(2)}) copy-start(f32[8,512]{1,0:T(8,128)S(1)} %get-tuple-element.12.hidden) | copy-start | bytes 49156
  33.8 2.7 %collective-permute-start = (bf16[64,8,512]{2,1,0:T(8,128)(2,1)S(1)}, bf16[64,8,512]{2,1,0:T(8,128)(2,1)S(1)}, u32[]{:S(2)}, u32[]{:S(2)}) collective-permute-start(bf16[64,8,512]{2,1,0:T(8,128)(2,1)S(1)} %all_to_all.10.own), channel_id=1, source_target_pairs={{0,1},{1,0},{2,3},{3,2},{4,5},{5,4},{6,7},{7,6},{8,9},{9,8},{10,11... | collective-permute-start | bytes 1572872 | tf_op jit(solution)/shard_map/ppermute | solution.py:132
  51.4 0.8 copy-start.4
  52.2 2.0 %collective-permute-start.1 = (bf16[64,8,512]{2,1,0:T(8,128)(2,1)S(1)}, bf16[64,8,512]{2,1,0:T(8,128)(2,1)S(1)}, u32[]{:S(2)}, u32[]{:S(2)}) collective-permute-start(bf16[64,8,512]{2,1,0:T(8,128)(2,1)S(1)} %get-tuple-element.11), channel_id=1, source_target_pairs={{0,1},{1,0},{2,3},{3,2},{4,5},{5,4},{6,7},{7,6},{8,9},{9,8},{10,11... | collective-permute-start | bytes 1572872 | tf_op jit(solution)/shard_map/ppermute | solution.py:132
  54.2 0.8 %copy-start.8 = (bf16[64,8,512]{2,1,0:T(8,128)(2,1)}, bf16[64,8,512]{2,1,0:T(8,128)(2,1)S(1)}, u32[]{:S(2)}) copy-start(bf16[64,8,512]{2,1,0:T(8,128)(2,1)S(1)} %collective-permute-done.1.b) | copy-start | bytes 1572868

commit v2 on v1

v2 whole, which is shorter than its diff:
```python
import jax
import jax.numpy as jnp
from jax import lax
from jax.experimental import pallas as pl
from jax.experimental.pallas import tpu as pltpu
from jax.sharding import Mesh, PartitionSpec as P

KV_HEADS = 8
GROUP = 4
HEADS = KV_HEADS * GROUP
HEAD_DIM = 128
RANK = 512
CTX = 1024
D = 4096
HIDDEN = 896
ROWS = 8
COLS = 512
CHIPS = 64
CHIP_AXES = ("z", "x", "y")
ALL_AXES = ("z", "x", "y", "core")
F32 = jnp.float32
BF16 = jnp.bfloat16
VMEM = pl.BlockSpec(memory_space=pltpu.VMEM)
SMEM = pl.BlockSpec(memory_space=pltpu.SMEM)
ANY = pl.BlockSpec(memory_space=pl.ANY)
MIB = 2**20
FIRST = 2048


def parts_of(x, n):
    out = []
    for _ in range(n):
        p = x.astype(BF16)
        out.append(p)
        x = x - p.astype(F32)
    return out


def dot_nt(a, b):
    return lax.dot_general(a, b, (((1,), (1,)), ((), ())), preferred_element_type=F32)


def dot(a, b):
    return jnp.dot(a, b, preferred_element_type=F32)


def to_rows(ref, scratch):
    for s in range(ROWS):
        scratch[s : s + 1, :] = ref[0:1, s * COLS : (s + 1) * COLS].astype(F32)
    return scratch[...]


def attend_kernel(
    length, query, hidden_in, gain, key_latent, value_latent, key_up, value_up,
    sent, hidden_out,
    rows_scratch, q_vmem, h_vmem, gain_vmem, kl_vmem, vl_vmem, ku_vmem, vu_vmem, small_sem, sem,
):
    small = [
        pltpu.make_async_copy(query, q_vmem, small_sem.at[0]),
        pltpu.make_async_copy(hidden_in, h_vmem, small_sem.at[1]),
        pltpu.make_async_copy(gain, gain_vmem, small_sem.at[2]),
    ]
    for c in small:
        c.start()
    big = [
        pltpu.make_async_copy(src, dst, sem.at[i])
        for i, (src, dst) in enumerate(
            ((key_up, ku_vmem), (key_latent.at[0], kl_vmem), (value_latent.at[0], vl_vmem), (value_up, vu_vmem))
        )
    ]
    big[0].start()
    big[1].start()
    for c in small:
        c.wait()
    big[2].start()
    big[3].start()

    q = to_rows(q_vmem, rows_scratch)
    kv_row = lax.broadcasted_iota(jnp.int32, (KV_HEADS, KV_HEADS * HEAD_DIM), 0)
    kv_col = lax.broadcasted_iota(jnp.int32, (KV_HEADS, KV_HEADS * HEAD_DIM), 1) // HEAD_DIM
    own_block = kv_row == kv_col
    spread = []
    for g in range(GROUP):
        piece = q[:, g * HEAD_DIM : (g + 1) * HEAD_DIM]
        spread.append(jnp.where(own_block, jnp.concatenate([piece] * KV_HEADS, axis=1), 0.0))
    spread = jnp.concatenate(spread, axis=0).astype(BF16)
    big[0].wait()
    folded = dot_nt(spread, ku_vmem[...])
    stacked = jnp.concatenate(parts_of(folded, 3), axis=0)
    big[1].wait()
    s3 = dot_nt(stacked, kl_vmem[...])
    scores = (s3[:HEADS] + s3[HEADS : 2 * HEADS] + s3[2 * HEADS :]) * HEAD_DIM ** (-0.5)
    usable = lax.broadcasted_iota(jnp.int32, (HEADS, CTX), 1) < length[0]
    scores = jnp.where(usable, scores, -1e30)
    peak = jnp.max(scores, axis=1, keepdims=True)
    weights = jnp.where(usable, jnp.exp(scores - peak), 0.0)
    total = jnp.sum(weights, axis=1, keepdims=True)
    w2 = jnp.concatenate(parts_of(weights, 2), axis=0)
    big[2].wait()
    l2 = dot(w2, vl_vmem[...])
    latent = (l2[:HEADS] + l2[HEADS:]) / total
    big[3].wait()
    v2 = dot(jnp.concatenate(parts_of(latent, 2), axis=0), vu_vmem[...])
    values = v2[:HEADS] + v2[HEADS:]
    attended = []
    for g in range(GROUP):
        mine = jnp.where(own_block, values[g * KV_HEADS : (g + 1) * KV_HEADS], 0.0)
        acc = mine[:, :HEAD_DIM]
        for k in range(1, KV_HEADS):
            acc = acc + mine[:, k * HEAD_DIM : (k + 1) * HEAD_DIM]
        attended.append(acc)
    attended = jnp.concatenate(attended, axis=1)
    hidden = (to_rows(h_vmem, rows_scratch) + attended).astype(BF16).astype(F32)
    hidden_out[...] = hidden
    square = jnp.sum(jnp.sum(hidden * hidden, axis=1, keepdims=True), axis=0, keepdims=True)
    scale = lax.rsqrt(square * (1.0 / D) + 1e-05)
    normed = (hidden * scale * gain_vmem[...].astype(F32).reshape(ROWS, COLS)).astype(BF16)
    sent[...] = jnp.broadcast_to(normed[None], sent.shape)


def gates_of(x, router, ids, parity, expert):
    shape = (2 * CHIPS, 2 * CHIPS)
    row = lax.broadcasted_iota(jnp.int32, shape, 0)
    other = (row >= CHIPS).astype(jnp.int32)
    token = 2 * (row - other * CHIPS) + (parity + other - 2 * parity * other)
    pick = (token == lax.broadcasted_iota(jnp.int32, shape, 1)).astype(F32).astype(BF16)
    wide_ids = jnp.concatenate([ids[...].astype(F32), jnp.zeros((6, 2 * CHIPS), F32)], axis=0).astype(BF16)
    mine = dot_nt(pick, wide_ids).astype(jnp.int32)
    first, second = mine[:, 0:1], mine[:, 1:2]
    logits = dot_nt(x, router[...])
    lane = lax.broadcasted_iota(jnp.int32, logits.shape, 1)
    logit_a = jnp.sum(jnp.where(lane == first, logits, 0.0), axis=1, keepdims=True)
    logit_b = jnp.sum(jnp.where(lane == second, logits, 0.0), axis=1, keepdims=True)
    peak = jnp.maximum(logit_a, logit_b)
    exp_a, exp_b = jnp.exp(logit_a - peak), jnp.exp(logit_b - peak)
    chosen = jnp.where(first == expert, exp_a, 0.0) + jnp.where(second == expert, exp_b, 0.0)
    return chosen / (exp_a + exp_b)


def load_kernel(after, gate, out, sem):
    copy = pltpu.make_async_copy(gate.at[0, pl.ds(0, FIRST)], out, sem)
    copy.start()
    copy.wait()


def expert_kernel(
    own, other, ids, router, gate_first, gate, up, down,
    out_own, out_other,
    rows, gate_rest, up_vmem, down_vmem, g_part, u_part, act, weight, sem,
):
    core = lax.axis_index("core")
    expert = 2 * lax.axis_index("y") + core
    step = pl.when(core >= 0)
    half = D // 2
    quarter = D // 4
    gate_copy = pltpu.make_async_copy(gate.at[0, pl.ds(FIRST, D - FIRST)], gate_rest, sem.at[0])
    up_copies = [
        pltpu.make_async_copy(
            up.at[0, pl.ds(j * half, half)], up_vmem.at[pl.ds(j * half, half)], sem.at[1 + j]
        )
        for j in range(2)
    ]
    down_copies = [
        pltpu.make_async_copy(
            down.at[0, :, pl.ds(j * quarter, quarter)], down_vmem.at[:, pl.ds(j * quarter, quarter)], sem.at[3 + j]
        )
        for j in range(4)
    ]
    for c in [gate_copy] + up_copies + down_copies:
        c.start()

    @step
    def _():
        rows[:CHIPS] = own[...].reshape(CHIPS, D)
        rows[CHIPS:] = other[...].reshape(CHIPS, D)

    @step
    def _():
        g_part[...] = dot(rows[:, :FIRST], gate_first[...])

    @step
    def _():
        weight[...] = jnp.broadcast_to(gates_of(rows[...], router, ids, core, expert), weight.shape)

    gate_copy.wait()

    @step
    def _():
        g_part[...] += dot(rows[:, FIRST:], gate_rest[...])

    up_copies[0].wait()

    @step
    def _():
        u_part[...] = dot(rows[:, :half], up_vmem[:half])

    up_copies[1].wait()

    @step
    def _():
        g = g_part[...]
        u = u_part[...] + dot(rows[:, half:], up_vmem[half:])
        act[...] = (g * jax.nn.sigmoid(g) * u).astype(BF16)

    for j, c in enumerate(down_copies):
        c.wait()

        @step
        def _(j=j):
            for s in (2 * j, 2 * j + 1):
                cols = slice(s * COLS, (s + 1) * COLS)
                rows[:, cols] = (dot(act[...], down_vmem[:, cols]) * weight[:, :1]).astype(BF16)

    @step
    def _():
        out_own[...] = rows[:CHIPS].reshape(out_own.shape)
        out_other[...] = rows[CHIPS:].reshape(out_other.shape)


def add_kernel(a, b, out):
    out[...] = (a[...].astype(F32) + b[...].astype(F32)).astype(BF16)


def finish_kernel(parts, hidden, out):
    total = jnp.sum(parts[...].astype(F32), axis=0) + hidden[...]
    for s in range(ROWS):
        out[0:1, s * COLS : (s + 1) * COLS] = total[s : s + 1, :].astype(BF16)


def swap_cores(x):
    return lax.ppermute(x, "core", [(0, 1), (1, 0)])


def params(mib):
    return pltpu.CompilerParams(vmem_limit_bytes=mib * MIB)


def in_vmem(x):
    return pltpu.with_memory_space_constraint(x, pltpu.VMEM)


def in_hbm(x):
    return pltpu.with_memory_space_constraint(x, pltpu.HBM)


def body(
    hidden_in, query, key_latent, value_latent, lengths, key_up, value_up,
    norm_gain, router_weight, route_ids, gate_weight, up_weight, down_weight,
):
    router = router_weight.T
    ids = route_ids.T
    block = (CHIPS, ROWS, COLS)
    token = jax.ShapeDtypeStruct(block, BF16)
    sent, hidden = pl.pallas_call(
        attend_kernel,
        out_shape=(token, jax.ShapeDtypeStruct((ROWS, COLS), F32)),
        in_specs=[SMEM] + [ANY] * 7,
        out_specs=(VMEM, VMEM),
        scratch_shapes=[
            pltpu.VMEM((ROWS, COLS), F32),
            pltpu.VMEM((1, D), BF16),
            pltpu.VMEM((1, D), BF16),
            pltpu.VMEM((D,), BF16),
            pltpu.VMEM((CTX, RANK), BF16),
            pltpu.VMEM((CTX, RANK), BF16),
            pltpu.VMEM((RANK, KV_HEADS * HEAD_DIM), BF16),
            pltpu.VMEM((RANK, KV_HEADS * HEAD_DIM), BF16),
            pltpu.SemaphoreType.DMA((3,)),
            pltpu.SemaphoreType.DMA((4,)),
        ],
        compiler_params=params(16),
        name="attend",
    )(
        lengths, in_hbm(query), in_hbm(hidden_in), in_hbm(norm_gain),
        in_hbm(key_latent), in_hbm(value_latent), in_hbm(key_up), in_hbm(value_up),
    )
    own = lax.all_to_all(sent, CHIP_AXES, 0, 0, tiled=True)
    other = swap_cores(own)
    gate_first = pl.pallas_call(
        load_kernel,
        out_shape=pltpu.VMEM((FIRST, HIDDEN), BF16),
        in_specs=[VMEM, ANY],
        out_specs=ANY,
        scratch_shapes=[pltpu.SemaphoreType.DMA],
        compiler_params=params(2),
        cost_estimate=pl.CostEstimate(flops=0, bytes_accessed=8 * MIB, transcendentals=0),
        name="load_gate",
    )(hidden, in_hbm(gate_weight))
    out_own, out_other = pl.pallas_call(
        expert_kernel,
        out_shape=(token, token),
        in_specs=[VMEM] * 5 + [ANY] * 3,
        out_specs=(VMEM, VMEM),
        scratch_shapes=[
            pltpu.VMEM((2 * CHIPS, D), BF16),
            pltpu.VMEM((D - FIRST, HIDDEN), BF16),
            pltpu.VMEM((D, HIDDEN), BF16),
            pltpu.VMEM((HIDDEN, D), BF16),
            pltpu.VMEM((2 * CHIPS, HIDDEN), F32),
            pltpu.VMEM((2 * CHIPS, HIDDEN), F32),
            pltpu.VMEM((2 * CHIPS, HIDDEN), BF16),
            pltpu.VMEM((2 * CHIPS, HEAD_DIM), F32),
            pltpu.SemaphoreType.DMA((7,)),
        ],
        compiler_params=params(32),
        name="experts",
    )(
        own, other, ids, router, in_vmem(gate_first),
        in_hbm(gate_weight), in_hbm(up_weight), in_hbm(down_weight),
    )
    from_other = swap_cores(out_other)
    summed = pl.pallas_call(
        add_kernel,
        out_shape=token,
        in_specs=[VMEM, VMEM],
        out_specs=VMEM,
        compiler_params=params(4),
        name="add_cores",
    )(out_own, from_other)
    parts = lax.all_to_all(summed, CHIP_AXES, 0, 0, tiled=True)
    return pl.pallas_call(
        finish_kernel,
        out_shape=jax.ShapeDtypeStruct((1, D), BF16),
        in_specs=[VMEM, VMEM],
        out_specs=VMEM,
        compiler_params=params(4),
        name="finish",
    )(parts, hidden)


def solution(mesh):
    fine = Mesh(mesh.devices.reshape(4, 4, 4, 2), ALL_AXES)
    in_specs = (
        P(ALL_AXES, None),
        P(ALL_AXES, None),
        P(ALL_AXES, None, None),
        P(ALL_AXES, None, None),
        P(ALL_AXES),
        P(),
        P(),
        P(),
        P(),
        P(),
        P(("y", "core"), None, ("z", "x")),
        P(("y", "core"), None, ("z", "x")),
        P(("y", "core"), ("z", "x"), None),
    )
    return jax.shard_map(
        body, mesh=fine, in_specs=in_specs, out_specs=P(ALL_AXES, None), check_vma=False
    )
```

time: 79.3 us -> 59.2 us (0.75)
  local copies, waits for them, and re-layouts: 11.2 us -> 0.01 us
  Pallas kernels: 20.3 us -> 13.1 us
  blocking collectives: 44 us -> 43 us
    unnamed x19 -> x4, local copies, waits for them, and re-layouts: 9.24 us -> 0.01 us
    pallas_call x1 -> x2, Pallas kernels: 14.9 us -> 9.02 us  [the longest x1 6.97 us: body(): pl.pallas_call(expert_kernel, out_shape=(token, token), in_specs=[VMEM] *...]
    pallas_call x1, Pallas kernels: 2.12 us -> 0.12 us  [body(): pl.pallas_call(add_kernel, out_shape=token, in_specs=[VMEM, VMEM], out_sp...]
    pallas_call x1, Pallas kernels: 1.56 us -> 3.24 us  [body(): pl.pallas_call(attend_kernel, out_shape=(token, jax.ShapeDtypeStruct((ROW...]
    reshape x2 -> x0, local copies, waits for them, and re-layouts: 1.52 us -> none  [the longest x1 0.81 us: body(): by_chip = route_ids.reshape(CHIPS, 2, 2)]
    all_to_all x1, blocking collectives: 19.5 us -> 18.4 us  [body(): parts = lax.all_to_all(summed, CHIP_AXES, 0, 0, tiled=True)]
    pallas_call x1, Pallas kernels: 1.73 us -> 0.68 us  [body(): pl.pallas_call(finish_kernel, out_shape=jax.ShapeDtypeStruct((1, D), BF16...]
  transfers between devices with their start and end apart: 2 -> 2, of which waited for: 1 -> 1; matrix products, arithmetic and copies ran while one was open for 3% -> 0% of each run, Pallas kernels for 0% -> 3%
where the time goes in v2:
time: 59.2 us; the launch traced here: 58.9 us
  blocking collectives  43 us (73%)
  Pallas kernels  13.1 us (22%)
  waiting for transfers between devices  1.54 us (3%)
  between operations  0.72 us (1%)
    all_to_all x1, blocking collectives, body(): own = lax.all_to_all(sent, CHIP_AXES, 0, 0, tiled=True)  24.6 us
    all_to_all x1, blocking collectives, body(): parts = lax.all_to_all(summed, CHIP_AXES, 0, 0, tiled=True)  18.4 us
    pallas_call x1, Pallas kernels, body(): pl.pallas_call(expert_kernel, out_shape=(token, token), in_specs=[VMEM] *...  6.97 us
    pallas_call x1, Pallas kernels, body(): pl.pallas_call(attend_kernel, out_shape=(token, jax.ShapeDtypeStruct((ROW...  3.24 us
    pallas_call x1, Pallas kernels, body(): pl.pallas_call(load_kernel, out_shape=pltpu.VMEM((FIRST, HIDDEN), BF16),...  2.05 us
    ppermute x2, waiting for transfers between devices, swap_cores(): return lax.ppermute(x, 'core', [(0, 1), (1, 0)])  1.54 us
  transfers between devices with their start and end apart: 2, of which 1 were waited for; matrix products, arithmetic and copies ran while one was open for 0% of the time, Pallas kernels for 3%

profile of v2, /device:TPU:0, one launch (start us, length us, event | category | flops | bytes accessed | tf_op | source)
XLA Modules:
  0.0 58.9 jit_solution(10617923330378648108)
XLA Ops:
  0.7 0.0 copy-start
  0.7 0.0 copy-start.1
  0.7 3.2 %attend.1 = (bf16[64,8,512]{2,1,0:T(8,128)(2,1)S(1)}, f32[8,512]{1,0:T(8,128)S(1)}) custom-call(s32[1]{0:T(128)S(6)} %copy.14.length, bf16[1,4096]{1,0:T(2,128)(2,1)} %query.1, bf16[1,4096]{1,0:T(2,128)(2,1)} %hidden_in.1, bf16[4096]{0:T(1024)(128)(2,1)} %gain.1, bf16[1,1024,512]{2,1,0:T(8,128)(2,1)} %key_latent.1, bf16[1,1024,512]{2,1,0:T(8,128)(2,1)} %value_latent.1, ...), custom_call_target="tpu_custom_call" | custom-call | tf_op jit(solution)/shard_map/attend/pallas_call | solution.py:254
  3.9 24.6 %all_to_all.10.own = bf16[64,8,512]{2,1,0:T(8,128)(2,1)S(1)} all-to-all(bf16[64,8,512]{2,1,0:T(8,128)(2,1)S(1)} %get-tuple-element.9), channel_id=1, replica_groups=mesh['z'=4,'x'=4,'y'=4,'core'=2] {'z','x','y'}, dimensions={0} | all-to-all | bytes 1048576 | tf_op jit(solution)/shard_map/all_to_all | solution.py:277
  28.5 0.0 collective-permute-start
  28.5 2.0 %load_gate.1.gate_first = bf16[2048,896]{1,0:T(8,128)(2,1)S(1)} custom-call(f32[8,512]{1,0:T(8,128)S(1)} %get-tuple-element.10.after.hidden, bf16[1,4096,896]{2,1,0:T(8,128)(2,1)} %gate.3), custom_call_target="tpu_custom_call" | custom-call | bytes 8388608 | tf_op jit(solution)/shard_map/load_gate/pallas_call | solution.py:279
  30.6 0.0 collective-permute-done.other
  30.6 0.0 copy-done
  30.6 0.0 copy-done.1
  30.6 7.0 %experts.1 = (bf16[64,8,512]{2,1,0:T(8,128)(2,1)S(1)}, bf16[64,8,512]{2,1,0:T(8,128)(2,1)S(1)}) custom-call(bf16[64,8,512]{2,1,0:T(8,128)(2,1)S(1)} %all_to_all.10.own, bf16[64,8,512]{2,1,0:T(8,128)(2,1)S(1)} %collective-permute-done.other, s32[2,128]{1,0:T(2,128)S(1)} %bitcast.3, bf16[8,4096]{1,0:T(8,128)(2,1)S(1)} %bitcast.2, ...), custom_call_target="tpu_custom_call" | custom-call | tf_op jit(solution)/shard_map/experts/pallas_call | solution.py:289
  37.6 0.6 collective-permute-start.1
  38.1 1.5 %collective-permute-done.1.b = bf16[64,8,512]{2,1,0:T(8,128)(2,1)S(1)} collective-permute-done((bf16[64,8,512]{2,1,0:T(8,128)(2,1)S(1)}, bf16[64,8,512]{2,1,0:T(8,128)(2,1)S(1)}, u32[]{:S(2)}, u32[]{:S(2)}) %collective-permute-start.1) | collective-permute-done | bytes 524320 | tf_op jit(solution)/shard_map/ppermute | solution.py:231
  39.7 0.1 add_cores.1
  39.8 18.4 %all_to_all.11.parts = bf16[64,8,512]{2,1,0:T(8,128)(2,1)S(1)} all-to-all(bf16[64,8,512]{2,1,0:T(8,128)(2,1)S(1)} %add_cores.1), channel_id=1, replica_groups=mesh['z'=4,'x'=4,'y'=4,'core'=2] {'z','x','y'}, dimensions={0} | all-to-all | bytes 1048576 | tf_op jit(solution)/shard_map/all_to_all | solution.py:320
  58.2 0.7 %finish.1 = bf16[1,4096]{1,0:T(2,128)(2,1)} custom-call(bf16[64,8,512]{2,1,0:T(8,128)(2,1)S(1)} %all_to_all.11.parts, f32[8,512]{1,0:T(8,128)S(1)} %get-tuple-element.10.after.hidden), custom_call_target="tpu_custom_call" | custom-call | tf_op jit(solution)/shard_map/finish/pallas_call | solution.py:321
Async XLA Ops:
  0.7 29.9 %copy-start = (bf16[4096,8]{0,1:T(8,128)(2,1)S(1)}, bf16[4096,8]{0,1:T(8,128)(2,1)}, u32[]{:S(2)}) copy-start(bf16[4096,8]{0,1:T(8,128)(2,1)} %param.21) | copy-start | bytes 196612
  0.7 29.9 %copy-start.1 = (s32[128,2]{0,1:T(2,128)S(1)}, s32[128,2]{0,1:T(2,128)}, u32[]{:S(2)}) copy-start(s32[128,2]{0,1:T(2,128)} %param.22) | copy-start | bytes 3076
  28.5 2.1 %collective-permute-start = (bf16[64,8,512]{2,1,0:T(8,128)(2,1)S(1)}, bf16[64,8,512]{2,1,0:T(8,128)(2,1)S(1)}, u32[]{:S(2)}, u32[]{:S(2)}) collective-permute-start(bf16[64,8,512]{2,1,0:T(8,128)(2,1)S(1)} %all_to_all.10.own), channel_id=1, source_target_pairs={{0,1},{1,0},{2,3},{3,2},{4,5},{5,4},{6,7},{7,6},{8,9},{9,8},{10,11... | collective-permute-start | bytes 1572872 | tf_op jit(solution)/shard_map/ppermute | solution.py:231
  37.6 2.1 %collective-permute-start.1 = (bf16[64,8,512]{2,1,0:T(8,128)(2,1)S(1)}, bf16[64,8,512]{2,1,0:T(8,128)(2,1)S(1)}, u32[]{:S(2)}, u32[]{:S(2)}) collective-permute-start(bf16[64,8,512]{2,1,0:T(8,128)(2,1)S(1)} %get-tuple-element.12), channel_id=1, source_target_pairs={{0,1},{1,0},{2,3},{3,2},{4,5},{5,4},{6,7},{7,6},{8,9},{9,8},{10,11... | collective-permute-start | bytes 1572872 | tf_op jit(solution)/shard_map/ppermute | solution.py:231

commit v3 on v2

--- a/solution.py
+++ b/solution.py
@@ -24,7 +24,6 @@
 SMEM = pl.BlockSpec(memory_space=pltpu.SMEM)
 ANY = pl.BlockSpec(memory_space=pl.ANY)
 MIB = 2**20
-FIRST = 2048
 
 
 def parts_of(x, n):
@@ -52,7 +51,7 @@
 
 def attend_kernel(
     length, query, hidden_in, gain, key_latent, value_latent, key_up, value_up,
-    sent, hidden_out,
+    normed_out, hidden_out,
     rows_scratch, q_vmem, h_vmem, gain_vmem, kl_vmem, vl_vmem, ku_vmem, vu_vmem, small_sem, sem,
 ):
     small = [
@@ -115,7 +114,7 @@
     square = jnp.sum(jnp.sum(hidden * hidden, axis=1, keepdims=True), axis=0, keepdims=True)
     scale = lax.rsqrt(square * (1.0 / D) + 1e-05)
     normed = (hidden * scale * gain_vmem[...].astype(F32).reshape(ROWS, COLS)).astype(BF16)
-    sent[...] = jnp.broadcast_to(normed[None], sent.shape)
+    normed_out[...] = normed
 
 
 def gates_of(x, router, ids, parity, expert):
@@ -137,84 +136,30 @@
     return chosen / (exp_a + exp_b)
 
 
-def load_kernel(after, gate, out, sem):
-    copy = pltpu.make_async_copy(gate.at[0, pl.ds(0, FIRST)], out, sem)
-    copy.start()
-    copy.wait()
-
-
-def expert_kernel(
-    own, other, ids, router, gate_first, gate, up, down,
-    out_own, out_other,
-    rows, gate_rest, up_vmem, down_vmem, g_part, u_part, act, weight, sem,
-):
+def pass_kernel(normed, *refs):
+    refs[-1][...] = normed[...]
+
+
+def spread_kernel(normed, *refs):
+    sent = refs[-1]
+    sent[...] = jnp.broadcast_to(normed[...][None], sent.shape)
+
+
+def expert_kernel(own, other, ids, router, gate, up, down, out_own, out_other, rows):
     core = lax.axis_index("core")
     expert = 2 * lax.axis_index("y") + core
-    step = pl.when(core >= 0)
-    half = D // 2
-    quarter = D // 4
-    gate_copy = pltpu.make_async_copy(gate.at[0, pl.ds(FIRST, D - FIRST)], gate_rest, sem.at[0])
-    up_copies = [
-        pltpu.make_async_copy(
-            up.at[0, pl.ds(j * half, half)], up_vmem.at[pl.ds(j * half, half)], sem.at[1 + j]
-        )
-        for j in range(2)
-    ]
-    down_copies = [
-        pltpu.make_async_copy(
-            down.at[0, :, pl.ds(j * quarter, quarter)], down_vmem.at[:, pl.ds(j * quarter, quarter)], sem.at[3 + j]
-        )
-        for j in range(4)
-    ]
-    for c in [gate_copy] + up_copies + down_copies:
-        c.start()
-
-    @step
-    def _():
-        rows[:CHIPS] = own[...].reshape(CHIPS, D)
-        rows[CHIPS:] = other[...].reshape(CHIPS, D)
-
-    @step
-    def _():
-        g_part[...] = dot(rows[:, :FIRST], gate_first[...])
-
-    @step
-    def _():
-        weight[...] = jnp.broadcast_to(gates_of(rows[...], router, ids, core, expert), weight.shape)
-
-    gate_copy.wait()
-
-    @step
-    def _():
-        g_part[...] += dot(rows[:, FIRST:], gate_rest[...])
-
-    up_copies[0].wait()
-
-    @step
-    def _():
-        u_part[...] = dot(rows[:, :half], up_vmem[:half])
-
-    up_copies[1].wait()
-
-    @step
-    def _():
-        g = g_part[...]
-        u = u_part[...] + dot(rows[:, half:], up_vmem[half:])
-        act[...] = (g * jax.nn.sigmoid(g) * u).astype(BF16)
-
-    for j, c in enumerate(down_copies):
-        c.wait()
-
-        @step
-        def _(j=j):
-            for s in (2 * j, 2 * j + 1):
-                cols = slice(s * COLS, (s + 1) * COLS)
-                rows[:, cols] = (dot(act[...], down_vmem[:, cols]) * weight[:, :1]).astype(BF16)
-
-    @step
-    def _():
-        out_own[...] = rows[:CHIPS].reshape(out_own.shape)
-        out_other[...] = rows[CHIPS:].reshape(out_other.shape)
+    rows[:CHIPS] = own[...].reshape(CHIPS, D)
+    rows[CHIPS:] = other[...].reshape(CHIPS, D)
+    x = rows[...]
+    weight = gates_of(x, router, ids, core, expert)
+    g = dot(x, gate[0])
+    u = dot(x, up[0])
+    act = (g * jax.nn.sigmoid(g) * u).astype(BF16)
+    for s in range(ROWS):
+        cols = slice(s * COLS, (s + 1) * COLS)
+        rows[:, cols] = (dot(act, down[0, :, cols]) * weight).astype(BF16)
+    out_own[...] = rows[:CHIPS].reshape(out_own.shape)
+    out_other[...] = rows[CHIPS:].reshape(out_other.shape)
 
 
 def add_kernel(a, b, out):
@@ -251,9 +196,12 @@
     ids = route_ids.T
     block = (CHIPS, ROWS, COLS)
     token = jax.ShapeDtypeStruct(block, BF16)
-    sent, hidden = pl.pallas_call(
+    normed, hidden = pl.pallas_call(
         attend_kernel,
-        out_shape=(token, jax.ShapeDtypeStruct((ROWS, COLS), F32)),
+        out_shape=(
+            jax.ShapeDtypeStruct((ROWS, COLS), BF16),
+            jax.ShapeDtypeStruct((ROWS, COLS), F32),
+        ),
         in_specs=[SMEM] + [ANY] * 7,
         out_specs=(VMEM, VMEM),
         scratch_shapes=[
@@ -274,40 +222,34 @@
         lengths, in_hbm(query), in_hbm(hidden_in), in_hbm(norm_gain),
         in_hbm(key_latent), in_hbm(value_latent), in_hbm(key_up), in_hbm(value_up),
     )
+    held = [in_hbm(w) for w in (gate_weight, up_weight, down_weight)]
+    normed = pl.pallas_call(
+        pass_kernel,
+        out_shape=jax.ShapeDtypeStruct((ROWS, COLS), BF16),
+        in_specs=[VMEM] + [ANY] * 3,
+        out_specs=VMEM,
+        compiler_params=params(2),
+        name="pass_on",
+    )(normed, *held)
+    sent = pl.pallas_call(
+        spread_kernel,
+        out_shape=token,
+        in_specs=[VMEM] + [ANY] * 3,
+        out_specs=VMEM,
+        compiler_params=params(2),
+        name="spread",
+    )(normed, *held)
     own = lax.all_to_all(sent, CHIP_AXES, 0, 0, tiled=True)
     other = swap_cores(own)
-    gate_first = pl.pallas_call(
-        load_kernel,
-        out_shape=pltpu.VMEM((FIRST, HIDDEN), BF16),
-        in_specs=[VMEM, ANY],
-        out_specs=ANY,
-        scratch_shapes=[pltpu.SemaphoreType.DMA],
-        compiler_params=params(2),
-        cost_estimate=pl.CostEstimate(flops=0, bytes_accessed=8 * MIB, transcendentals=0),
-        name="load_gate",
-    )(hidden, in_hbm(gate_weight))
     out_own, out_other = pl.pallas_call(
         expert_kernel,
         out_shape=(token, token),
-        in_specs=[VMEM] * 5 + [ANY] * 3,
+        in_specs=[VMEM] * 7,
         out_specs=(VMEM, VMEM),
-        scratch_shapes=[
-            pltpu.VMEM((2 * CHIPS, D), BF16),
-            pltpu.VMEM((D - FIRST, HIDDEN), BF16),
-            pltpu.VMEM((D, HIDDEN), BF16),
-            pltpu.VMEM((HIDDEN, D), BF16),
-            pltpu.VMEM((2 * CHIPS, HIDDEN), F32),
-            pltpu.VMEM((2 * CHIPS, HIDDEN), F32),
-            pltpu.VMEM((2 * CHIPS, HIDDEN), BF16),
-            pltpu.VMEM((2 * CHIPS, HEAD_DIM), F32),
-            pltpu.SemaphoreType.DMA((7,)),
-        ],
-        compiler_params=params(32),
+        scratch_shapes=[pltpu.VMEM((2 * CHIPS, D), BF16)],
+        compiler_params=params(12),
         name="experts",
-    )(
-        own, other, ids, router, in_vmem(gate_first),
-        in_hbm(gate_weight), in_hbm(up_weight), in_hbm(down_weight),
-    )
+    )(own, other, ids, router, in_vmem(gate_weight), in_vmem(up_weight), in_vmem(down_weight))
     from_other = swap_cores(out_other)
     summed = pl.pallas_call(
         add_kernel,

time: 59.2 us -> 56 us (0.946)
  Pallas kernels: 13.1 us -> 8 us
  waiting for transfers between devices: 1.54 us -> 3.69 us
    pallas_call x1, Pallas kernels: 6.97 us -> 3.96 us  [body(): pl.pallas_call(expert_kernel, out_shape=(token, token), in_specs=[VMEM] *...]
    ppermute x2, waiting for transfers between devices: 1.54 us -> 3.69 us  [swap_cores(): return lax.ppermute(x, 'core', [(0, 1), (1, 0)])]
    pallas_call x2 -> x3, Pallas kernels: 5.29 us -> 3.23 us  [the longest x1 3.19 us: body(): pl.pallas_call(attend_kernel, out_shape=(jax.ShapeDtypeStruct((ROWS, COLS...]
  transfers between devices with their start and end apart: 2 -> 2, of which waited for: 1 -> 2; matrix products, arithmetic and copies ran while one was open for 0% -> 0% of each run, Pallas kernels for 3% -> 0%
where the time goes in v3:
time: 56 us; the launch traced here: 55.8 us
  blocking collectives  43 us (77%)
  Pallas kernels  8 us (14%)
  waiting for transfers between devices  3.69 us (7%)
  between operations  0.82 us (1%)
    all_to_all x1, blocking collectives, body(): own = lax.all_to_all(sent, CHIP_AXES, 0, 0, tiled=True)  24.8 us
    all_to_all x1, blocking collectives, body(): parts = lax.all_to_all(summed, CHIP_AXES, 0, 0, tiled=True)  18.2 us
    pallas_call x1, Pallas kernels, body(): pl.pallas_call(expert_kernel, out_shape=(token, token), in_specs=[VMEM] *...  3.96 us
    ppermute x2, waiting for transfers between devices, swap_cores(): return lax.ppermute(x, 'core', [(0, 1), (1, 0)])  3.69 us
    pallas_call x1, Pallas kernels, body(): pl.pallas_call(attend_kernel, out_shape=(jax.ShapeDtypeStruct((ROWS, COLS...  3.19 us
  transfers between devices with their start and end apart: 2, of which 2 were waited for; matrix products, arithmetic and copies ran while one was open for 0% of the time, Pallas kernels for 0%

profile of v3, /device:TPU:0, one launch (start us, length us, event | category | flops | bytes accessed | tf_op | source)
XLA Modules:
  0.0 55.8 jit_solution(13188848416335631532)
XLA Ops:
  0.7 3.2 %attend.1 = (bf16[8,512]{1,0:T(8,128)(2,1)S(1)}, f32[8,512]{1,0:T(8,128)S(1)}) custom-call(s32[1]{0:T(128)S(6)} %copy.14.length, bf16[1,4096]{1,0:T(2,128)(2,1)} %query.1, bf16[1,4096]{1,0:T(2,128)(2,1)} %hidden_in.1, bf16[4096]{0:T(1024)(128)(2,1)} %gain.1, bf16[1,1024,512]{2,1,0:T(8,128)(2,1)} %key_latent.1, bf16[1,1024,512]{2,1,0:T(8,128)(2,1)} %value_latent.1, ...), custom_call_target="tpu_custom_call" | custom-call | tf_op jit(solution)/shard_map/attend/pallas_call | solution.py:199
  3.9 0.0 slice-start
  3.9 0.0 slice-start.2
  3.9 0.0 slice-start.4
  3.9 0.0 slice-start.1
  3.9 0.0 slice-start.3
  3.9 0.0 slice-start.5
  3.9 0.0 copy-start
  4.0 0.0 copy-start.1
  4.0 24.8 %all_to_all.10.own = bf16[64,8,512]{2,1,0:T(8,128)(2,1)S(1)} all-to-all(bf16[64,8,512]{2,1,0:T(8,128)(2,1)S(1)} %spread.1), channel_id=1, replica_groups=mesh['z'=4,'x'=4,'y'=4,'core'=2] {'z','x','y'}, dimensions={0} | all-to-all | bytes 1048576 | tf_op jit(solution)/shard_map/all_to_all | solution.py:242
  28.8 0.0 collective-permute-start
  28.8 1.9 %collective-permute-done.other = bf16[64,8,512]{2,1,0:T(8,128)(2,1)S(1)} collective-permute-done((bf16[64,8,512]{2,1,0:T(8,128)(2,1)S(1)}, bf16[64,8,512]{2,1,0:T(8,128)(2,1)S(1)}, u32[]{:S(2)}, u32[]{:S(2)}) %collective-permute-start) | collective-permute-done | bytes 524320 | tf_op jit(solution)/shard_map/ppermute | solution.py:176
  30.8 0.0 slice-done
  30.8 0.0 slice-done.2
  30.8 0.0 slice-done.4
  30.8 0.0 slice-done.1
  30.8 0.0 slice-done.3
  30.8 0.0 slice-done.5
  30.8 0.0 copy-done
  30.8 0.0 copy-done.1
  30.8 4.0 %experts.1 = (bf16[64,8,512]{2,1,0:T(8,128)(2,1)S(1)}, bf16[64,8,512]{2,1,0:T(8,128)(2,1)S(1)}) custom-call(bf16[64,8,512]{2,1,0:T(8,128)(2,1)S(1)} %all_to_all.10.own, bf16[64,8,512]{2,1,0:T(8,128)(2,1)S(1)} %collective-permute-done.other, s32[2,128]{1,0:T(2,128)S(1)} %bitcast.9, bf16[8,4096]{1,0:T(8,128)(2,1)S(1)} %bitcast.8, ...), custom_call_target="tpu_custom_call" | custom-call | tf_op jit(solution)/shard_map/experts/pallas_call | solution.py:244
  34.8 0.2 collective-permute-start.1
  35.0 1.8 %collective-permute-done.1.b = bf16[64,8,512]{2,1,0:T(8,128)(2,1)S(1)} collective-permute-done((bf16[64,8,512]{2,1,0:T(8,128)(2,1)S(1)}, bf16[64,8,512]{2,1,0:T(8,128)(2,1)S(1)}, u32[]{:S(2)}, u32[]{:S(2)}) %collective-permute-start.1) | collective-permute-done | bytes 524320 | tf_op jit(solution)/shard_map/ppermute | solution.py:176
  36.8 0.1 add_cores.1
  36.9 18.2 %all_to_all.11.parts = bf16[64,8,512]{2,1,0:T(8,128)(2,1)S(1)} all-to-all(bf16[64,8,512]{2,1,0:T(8,128)(2,1)S(1)} %add_cores.1), channel_id=1, replica_groups=mesh['z'=4,'x'=4,'y'=4,'core'=2] {'z','x','y'}, dimensions={0} | all-to-all | bytes 1048576 | tf_op jit(solution)/shard_map/all_to_all | solution.py:262
  55.1 0.7 %finish.1 = bf16[1,4096]{1,0:T(2,128)(2,1)} custom-call(bf16[64,8,512]{2,1,0:T(8,128)(2,1)S(1)} %all_to_all.11.parts, f32[8,512]{1,0:T(8,128)S(1)} %get-tuple-element.12.hidden), custom_call_target="tpu_custom_call" | custom-call | tf_op jit(solution)/shard_map/finish/pallas_call | solution.py:263
  (5 shorter events, 0.0 us)
Async XLA Ops:
  3.9 26.9 %slice-start = ((s8[7340032]{0:T(1024)(128)(4,1)}), s8[4194304]{0:T(1024)(128)(4,1)S(1)}, s32[]{:S(2)}) async-start(s8[7340032]{0:T(1024)(128)(4,1)} %bitcast.2), calls=%async_computation.2 | async-start | bytes 8388608
  3.9 26.9 %slice-start.2 = ((s8[7340032]{0:T(1024)(128)(4,1)}), s8[4194304]{0:T(1024)(128)(4,1)S(1)}, s32[]{:S(2)}) async-start(s8[7340032]{0:T(1024)(128)(4,1)} %bitcast.4), calls=%async_computation.4 | async-start | bytes 8388608
  3.9 26.9 %slice-start.4 = ((s8[7340032]{0:T(1024)(128)(4,1)}), s8[4194304]{0:T(1024)(128)(4,1)S(1)}, s32[]{:S(2)}) async-start(s8[7340032]{0:T(1024)(128)(4,1)} %bitcast.6), calls=%async_computation.6 | async-start | bytes 8388608
  3.9 26.9 %slice-start.1 = ((s8[7340032]{0:T(1024)(128)(4,1)}), s8[3145728]{0:T(1024)(128)(4,1)S(1)}, s32[]{:S(2)}) async-start(s8[7340032]{0:T(1024)(128)(4,1)} %bitcast.2), calls=%async_computation.3 | async-start | bytes 6291456
  3.9 26.9 %slice-start.3 = ((s8[7340032]{0:T(1024)(128)(4,1)}), s8[3145728]{0:T(1024)(128)(4,1)S(1)}, s32[]{:S(2)}) async-start(s8[7340032]{0:T(1024)(128)(4,1)} %bitcast.4), calls=%async_computation.5 | async-start | bytes 6291456
  3.9 26.9 %slice-start.5 = ((s8[7340032]{0:T(1024)(128)(4,1)}), s8[3145728]{0:T(1024)(128)(4,1)S(1)}, s32[]{:S(2)}) async-start(s8[7340032]{0:T(1024)(128)(4,1)} %bitcast.6), calls=%async_computation.7 | async-start | bytes 6291456
  3.9 26.9 %copy-start = (bf16[4096,8]{0,1:T(8,128)(2,1)S(1)}, bf16[4096,8]{0,1:T(8,128)(2,1)}, u32[]{:S(2)}) copy-start(bf16[4096,8]{0,1:T(8,128)(2,1)} %param.21) | copy-start | bytes 196612
  4.0 26.9 %copy-start.1 = (s32[128,2]{0,1:T(2,128)S(1)}, s32[128,2]{0,1:T(2,128)}, u32[]{:S(2)}) copy-start(s32[128,2]{0,1:T(2,128)} %param.22) | copy-start | bytes 3076
  28.8 1.9 %collective-permute-start = (bf16[64,8,512]{2,1,0:T(8,128)(2,1)S(1)}, bf16[64,8,512]{2,1,0:T(8,128)(2,1)S(1)}, u32[]{:S(2)}, u32[]{:S(2)}) collective-permute-start(bf16[64,8,512]{2,1,0:T(8,128)(2,1)S(1)} %all_to_all.10.own), channel_id=1, source_target_pairs={{0,1},{1,0},{2,3},{3,2},{4,5},{5,4},{6,7},{7,6},{8,9},{9,8},{10,11... | collective-permute-start | bytes 1572872 | tf_op jit(solution)/shard_map/ppermute | solution.py:176
  34.8 2.0 %collective-permute-start.1 = (bf16[64,8,512]{2,1,0:T(8,128)(2,1)S(1)}, bf16[64,8,512]{2,1,0:T(8,128)(2,1)S(1)}, u32[]{:S(2)}, u32[]{:S(2)}) collective-permute-start(bf16[64,8,512]{2,1,0:T(8,128)(2,1)S(1)} %get-tuple-element.11), channel_id=1, source_target_pairs={{0,1},{1,0},{2,3},{3,2},{4,5},{5,4},{6,7},{7,6},{8,9},{9,8},{10,11... | collective-permute-start | bytes 1572872 | tf_op jit(solution)/shard_map/ppermute | solution.py:176

commit v4 on v3

--- a/solution.py
+++ b/solution.py
@@ -16,7 +16,7 @@
 ROWS = 8
 COLS = 512
 CHIPS = 64
-CHIP_AXES = ("z", "x", "y")
+CHIP_AXES = ('x', 'y', 'z')
 ALL_AXES = ("z", "x", "y", "core")
 F32 = jnp.float32
 BF16 = jnp.bfloat16
@@ -59,18 +59,15 @@
         pltpu.make_async_copy(hidden_in, h_vmem, small_sem.at[1]),
         pltpu.make_async_copy(gain, gain_vmem, small_sem.at[2]),
     ]
-    for c in small:
-        c.start()
     big = [
         pltpu.make_async_copy(src, dst, sem.at[i])
         for i, (src, dst) in enumerate(
             ((key_up, ku_vmem), (key_latent.at[0], kl_vmem), (value_latent.at[0], vl_vmem), (value_up, vu_vmem))
         )
     ]
-    big[0].start()
-    big[1].start()
-    for c in small:
-        c.wait()
+    for c in (small[0], big[0], big[1], small[1], small[2]):
+        c.start()
+    small[0].wait()
     big[2].start()
     big[3].start()
 
@@ -109,6 +106,8 @@
             acc = acc + mine[:, k * HEAD_DIM : (k + 1) * HEAD_DIM]
         attended.append(acc)
     attended = jnp.concatenate(attended, axis=1)
+    small[1].wait()
+    small[2].wait()
     hidden = (to_rows(h_vmem, rows_scratch) + attended).astype(BF16).astype(F32)
     hidden_out[...] = hidden
     square = jnp.sum(jnp.sum(hidden * hidden, axis=1, keepdims=True), axis=0, keepdims=True)
@@ -121,7 +120,10 @@
     shape = (2 * CHIPS, 2 * CHIPS)
     row = lax.broadcasted_iota(jnp.int32, shape, 0)
     other = (row >= CHIPS).astype(jnp.int32)
-    token = 2 * (row - other * CHIPS) + (parity + other - 2 * parity * other)
+    place = row - other * CHIPS
+    digits = dict(zip(CHIP_AXES, (place // 16, (place // 4) % 4, place % 4)))
+    chip = digits["z"] * 16 + digits["x"] * 4 + digits["y"]
+    token = 2 * chip + (parity + other - 2 * parity * other)
     pick = (token == lax.broadcasted_iota(jnp.int32, shape, 1)).astype(F32).astype(BF16)
     wide_ids = jnp.concatenate([ids[...].astype(F32), jnp.zeros((6, 2 * CHIPS), F32)], axis=0).astype(BF16)
     mine = dot_nt(pick, wide_ids).astype(jnp.int32)

time: 56 us -> 55.7 us (level)
  no operation moved by 1% of the time
where the time goes in v4:
time: 55.7 us; the launch traced here: 55.5 us
  blocking collectives  42.8 us (77%)
  Pallas kernels  7.9 us (14%)
  waiting for transfers between devices  3.69 us (7%)
  between operations  0.82 us (1%)
    all_to_all x1, blocking collectives, body(): own = lax.all_to_all(sent, CHIP_AXES, 0, 0, tiled=True)  24.7 us
    all_to_all x1, blocking collectives, body(): parts = lax.all_to_all(summed, CHIP_AXES, 0, 0, tiled=True)  18.1 us
    pallas_call x1, Pallas kernels, body(): pl.pallas_call(expert_kernel, out_shape=(token, token), in_specs=[VMEM] *...  3.97 us
    ppermute x2, waiting for transfers between devices, swap_cores(): return lax.ppermute(x, 'core', [(0, 1), (1, 0)])  3.69 us
    pallas_call x1, Pallas kernels, body(): pl.pallas_call(attend_kernel, out_shape=(jax.ShapeDtypeStruct((ROWS, COLS...  3.09 us
  transfers between devices with their start and end apart: 2, of which 2 were waited for; matrix products, arithmetic and copies ran while one was open for 0% of the time, Pallas kernels for 0%

profile of v4, /device:TPU:0, one launch (start us, length us, event | category | flops | bytes accessed | tf_op | source)
XLA Modules:
  0.0 55.5 jit_solution(8857788270419262319)
XLA Ops:
  0.7 3.1 %attend.1 = (bf16[8,512]{1,0:T(8,128)(2,1)S(1)}, f32[8,512]{1,0:T(8,128)S(1)}) custom-call(s32[1]{0:T(128)S(6)} %copy.14.length, bf16[1,4096]{1,0:T(2,128)(2,1)} %query.1, bf16[1,4096]{1,0:T(2,128)(2,1)} %hidden_in.1, bf16[4096]{0:T(1024)(128)(2,1)} %gain.1, bf16[1,1024,512]{2,1,0:T(8,128)(2,1)} %key_latent.1, bf16[1,1024,512]{2,1,0:T(8,128)(2,1)} %value_latent.1, ...), custom_call_target="tpu_custom_call" | custom-call | tf_op jit(solution)/shard_map/attend/pallas_call | solution.py:201
  3.7 0.0 slice-start
  3.8 0.0 slice-start.2
  3.8 0.0 slice-start.4
  3.8 0.0 slice-start.1
  3.8 0.0 slice-start.3
  3.8 0.0 slice-start.5
  3.8 0.0 copy-start
  3.9 0.0 copy-start.1
  3.9 24.7 %all_to_all.10.own = bf16[64,8,512]{2,1,0:T(8,128)(2,1)S(1)} all-to-all(bf16[64,8,512]{2,1,0:T(8,128)(2,1)S(1)} %spread.1), channel_id=1, replica_groups=mesh['z'=4,'x'=4,'y'=4,'core'=2] {'x','y','z'}, dimensions={0} | all-to-all | bytes 1048576 | tf_op jit(solution)/shard_map/all_to_all | solution.py:244
  28.6 0.0 collective-permute-start
  28.6 1.9 %collective-permute-done.other = bf16[64,8,512]{2,1,0:T(8,128)(2,1)S(1)} collective-permute-done((bf16[64,8,512]{2,1,0:T(8,128)(2,1)S(1)}, bf16[64,8,512]{2,1,0:T(8,128)(2,1)S(1)}, u32[]{:S(2)}, u32[]{:S(2)}) %collective-permute-start) | collective-permute-done | bytes 524320 | tf_op jit(solution)/shard_map/ppermute | solution.py:178
  30.5 0.0 slice-done
  30.5 0.0 slice-done.2
  30.5 0.0 slice-done.4
  30.5 0.0 slice-done.1
  30.5 0.0 slice-done.3
  30.5 0.0 slice-done.5
  30.5 0.0 copy-done
  30.5 0.0 copy-done.1
  30.6 4.0 %experts.1 = (bf16[64,8,512]{2,1,0:T(8,128)(2,1)S(1)}, bf16[64,8,512]{2,1,0:T(8,128)(2,1)S(1)}) custom-call(bf16[64,8,512]{2,1,0:T(8,128)(2,1)S(1)} %all_to_all.10.own, bf16[64,8,512]{2,1,0:T(8,128)(2,1)S(1)} %collective-permute-done.other, s32[2,128]{1,0:T(2,128)S(1)} %bitcast.9, bf16[8,4096]{1,0:T(8,128)(2,1)S(1)} %bitcast.8, ...), custom_call_target="tpu_custom_call" | custom-call | tf_op jit(solution)/shard_map/experts/pallas_call | solution.py:246
  34.5 0.2 collective-permute-start.1
  34.8 1.8 %collective-permute-done.1.b = bf16[64,8,512]{2,1,0:T(8,128)(2,1)S(1)} collective-permute-done((bf16[64,8,512]{2,1,0:T(8,128)(2,1)S(1)}, bf16[64,8,512]{2,1,0:T(8,128)(2,1)S(1)}, u32[]{:S(2)}, u32[]{:S(2)}) %collective-permute-start.1) | collective-permute-done | bytes 524320 | tf_op jit(solution)/shard_map/ppermute | solution.py:178
  36.5 0.1 add_cores.1
  36.7 18.1 %all_to_all.11.parts = bf16[64,8,512]{2,1,0:T(8,128)(2,1)S(1)} all-to-all(bf16[64,8,512]{2,1,0:T(8,128)(2,1)S(1)} %add_cores.1), channel_id=1, replica_groups=mesh['z'=4,'x'=4,'y'=4,'core'=2] {'x','y','z'}, dimensions={0} | all-to-all | bytes 1048576 | tf_op jit(solution)/shard_map/all_to_all | solution.py:264
  54.8 0.7 %finish.1 = bf16[1,4096]{1,0:T(2,128)(2,1)} custom-call(bf16[64,8,512]{2,1,0:T(8,128)(2,1)S(1)} %all_to_all.11.parts, f32[8,512]{1,0:T(8,128)S(1)} %get-tuple-element.12.hidden), custom_call_target="tpu_custom_call" | custom-call | tf_op jit(solution)/shard_map/finish/pallas_call | solution.py:265
  (5 shorter events, 0.0 us)
Async XLA Ops:
  3.7 26.7 %slice-start = ((s8[7340032]{0:T(1024)(128)(4,1)}), s8[4194304]{0:T(1024)(128)(4,1)S(1)}, s32[]{:S(2)}) async-start(s8[7340032]{0:T(1024)(128)(4,1)} %bitcast.2), calls=%async_computation.2 | async-start | bytes 8388608
  3.8 26.7 %slice-start.2 = ((s8[7340032]{0:T(1024)(128)(4,1)}), s8[4194304]{0:T(1024)(128)(4,1)S(1)}, s32[]{:S(2)}) async-start(s8[7340032]{0:T(1024)(128)(4,1)} %bitcast.4), calls=%async_computation.4 | async-start | bytes 8388608
  3.8 26.7 %slice-start.4 = ((s8[7340032]{0:T(1024)(128)(4,1)}), s8[4194304]{0:T(1024)(128)(4,1)S(1)}, s32[]{:S(2)}) async-start(s8[7340032]{0:T(1024)(128)(4,1)} %bitcast.6), calls=%async_computation.6 | async-start | bytes 8388608
  3.8 26.7 %slice-start.1 = ((s8[7340032]{0:T(1024)(128)(4,1)}), s8[3145728]{0:T(1024)(128)(4,1)S(1)}, s32[]{:S(2)}) async-start(s8[7340032]{0:T(1024)(128)(4,1)} %bitcast.2), calls=%async_computation.3 | async-start | bytes 6291456
  3.8 26.7 %slice-start.3 = ((s8[7340032]{0:T(1024)(128)(4,1)}), s8[3145728]{0:T(1024)(128)(4,1)S(1)}, s32[]{:S(2)}) async-start(s8[7340032]{0:T(1024)(128)(4,1)} %bitcast.4), calls=%async_computation.5 | async-start | bytes 6291456
  3.8 26.7 %slice-start.5 = ((s8[7340032]{0:T(1024)(128)(4,1)}), s8[3145728]{0:T(1024)(128)(4,1)S(1)}, s32[]{:S(2)}) async-start(s8[7340032]{0:T(1024)(128)(4,1)} %bitcast.6), calls=%async_computation.7 | async-start | bytes 6291456
  3.8 26.7 %copy-start = (bf16[4096,8]{0,1:T(8,128)(2,1)S(1)}, bf16[4096,8]{0,1:T(8,128)(2,1)}, u32[]{:S(2)}) copy-start(bf16[4096,8]{0,1:T(8,128)(2,1)} %param.21) | copy-start | bytes 196612
  3.9 26.7 %copy-start.1 = (s32[128,2]{0,1:T(2,128)S(1)}, s32[128,2]{0,1:T(2,128)}, u32[]{:S(2)}) copy-start(s32[128,2]{0,1:T(2,128)} %param.22) | copy-start | bytes 3076
  28.6 1.9 %collective-permute-start = (bf16[64,8,512]{2,1,0:T(8,128)(2,1)S(1)}, bf16[64,8,512]{2,1,0:T(8,128)(2,1)S(1)}, u32[]{:S(2)}, u32[]{:S(2)}) collective-permute-start(bf16[64,8,512]{2,1,0:T(8,128)(2,1)S(1)} %all_to_all.10.own), channel_id=1, source_target_pairs={{0,1},{1,0},{2,3},{3,2},{4,5},{5,4},{6,7},{7,6},{8,9},{9,8},{10,11... | collective-permute-start | bytes 1572872 | tf_op jit(solution)/shard_map/ppermute | solution.py:178
  34.5 2.0 %collective-permute-start.1 = (bf16[64,8,512]{2,1,0:T(8,128)(2,1)S(1)}, bf16[64,8,512]{2,1,0:T(8,128)(2,1)S(1)}, u32[]{:S(2)}, u32[]{:S(2)}) collective-permute-start(bf16[64,8,512]{2,1,0:T(8,128)(2,1)S(1)} %get-tuple-element.11), channel_id=1, source_target_pairs={{0,1},{1,0},{2,3},{3,2},{4,5},{5,4},{6,7},{7,6},{8,9},{9,8},{10,11... | collective-permute-start | bytes 1572872 | tf_op jit(solution)/shard_map/ppermute | solution.py:178

commit v5 on v4

--- a/solution.py
+++ b/solution.py
@@ -117,13 +117,10 @@
 
 
 def gates_of(x, router, ids, parity, expert):
-    shape = (2 * CHIPS, 2 * CHIPS)
-    row = lax.broadcasted_iota(jnp.int32, shape, 0)
-    other = (row >= CHIPS).astype(jnp.int32)
-    place = row - other * CHIPS
+    shape = (CHIPS, 2 * CHIPS)
+    place = lax.broadcasted_iota(jnp.int32, shape, 0)
     digits = dict(zip(CHIP_AXES, (place // 16, (place // 4) % 4, place % 4)))
-    chip = digits["z"] * 16 + digits["x"] * 4 + digits["y"]
-    token = 2 * chip + (parity + other - 2 * parity * other)
+    token = 2 * (digits["z"] * 16 + digits["x"] * 4 + digits["y"]) + parity
     pick = (token == lax.broadcasted_iota(jnp.int32, shape, 1)).astype(F32).astype(BF16)
     wide_ids = jnp.concatenate([ids[...].astype(F32), jnp.zeros((6, 2 * CHIPS), F32)], axis=0).astype(BF16)
     mine = dot_nt(pick, wide_ids).astype(jnp.int32)
@@ -147,21 +144,37 @@
     sent[...] = jnp.broadcast_to(normed[...][None], sent.shape)
 
 
-def expert_kernel(own, other, ids, router, gate, up, down, out_own, out_other, rows):
+def own_kernel(own, ids, router, rows_out, weight_out):
     core = lax.axis_index("core")
-    expert = 2 * lax.axis_index("y") + core
-    rows[:CHIPS] = own[...].reshape(CHIPS, D)
+    x = own[...].reshape(CHIPS, D)
+    rows_out[...] = x
+    weight = gates_of(x, router, ids, core, 2 * lax.axis_index("y") + core)
+    weight_out[...] = jnp.broadcast_to(weight, weight_out.shape)
+
+
+def expert_kernel(
+    own_rows, own_weight, other, ids, router, gate, up, down,
+    out_own, out_other, rows,
+):
+    core = lax.axis_index("core")
+    rows[:CHIPS] = own_rows[...]
     rows[CHIPS:] = other[...].reshape(CHIPS, D)
     x = rows[...]
-    weight = gates_of(x, router, ids, core, expert)
+    other_weight = gates_of(rows[CHIPS:], router, ids, 1 - core, 2 * lax.axis_index("y") + core)
+    weight = jnp.concatenate([own_weight[:, :1], other_weight], axis=0)
     g = dot(x, gate[0])
     u = dot(x, up[0])
     act = (g * jax.nn.sigmoid(g) * u).astype(BF16)
     for s in range(ROWS):
         cols = slice(s * COLS, (s + 1) * COLS)
-        rows[:, cols] = (dot(act, down[0, :, cols]) * weight).astype(BF16)
-    out_own[...] = rows[:CHIPS].reshape(out_own.shape)
+        part = (dot(act, down[0, :, cols]) * weight).astype(BF16)
+        out_own[:, cols] = part[:CHIPS]
+        rows[CHIPS:, cols] = part[CHIPS:]
     out_other[...] = rows[CHIPS:].reshape(out_other.shape)
+
+
+def blocks_kernel(rows, out):
+    out[...] = rows[...].reshape(out.shape)
 
 
 def add_kernel(a, b, out):
@@ -243,16 +256,40 @@
     )(normed, *held)
     own = lax.all_to_all(sent, CHIP_AXES, 0, 0, tiled=True)
     other = swap_cores(own)
+    own_rows, own_weight = pl.pallas_call(
+        own_kernel,
+        out_shape=(
+            jax.ShapeDtypeStruct((CHIPS, D), BF16),
+            jax.ShapeDtypeStruct((CHIPS, HEAD_DIM), F32),
+        ),
+        in_specs=[VMEM] * 3,
+        out_specs=(VMEM,) * 2,
+        compiler_params=params(4),
+        cost_estimate=pl.CostEstimate(flops=0, bytes_accessed=2 * MIB, transcendentals=0),
+        name="own_rows",
+    )(own, ids, router)
     out_own, out_other = pl.pallas_call(
         expert_kernel,
-        out_shape=(token, token),
-        in_specs=[VMEM] * 7,
+        out_shape=(jax.ShapeDtypeStruct((CHIPS, D), BF16), token),
+        in_specs=[VMEM] * 8,
         out_specs=(VMEM, VMEM),
         scratch_shapes=[pltpu.VMEM((2 * CHIPS, D), BF16)],
         compiler_params=params(12),
         name="experts",
-    )(own, other, ids, router, in_vmem(gate_weight), in_vmem(up_weight), in_vmem(down_weight))
+    )(
+        own_rows, own_weight, other, ids, router,
+        in_vmem(gate_weight), in_vmem(up_weight), in_vmem(down_weight),
+    )
     from_other = swap_cores(out_other)
+    out_own = pl.pallas_call(
+        blocks_kernel,
+        out_shape=token,
+        in_specs=[VMEM],
+        out_specs=VMEM,
+        compiler_params=params(4),
+        cost_estimate=pl.CostEstimate(flops=0, bytes_accessed=2 * MIB, transcendentals=0),
+        name="own_blocks",
+    )(out_own)
     summed = pl.pallas_call(
         add_kernel,
         out_shape=token,

time: 55.7 us -> 55.4 us (level)
  waiting for transfers between devices: 3.69 us -> 2.97 us
    ppermute x2, waiting for transfers between devices: 3.69 us -> 2.97 us  [swap_cores(): return lax.ppermute(x, 'core', [(0, 1), (1, 0)])]
    pallas_call x1 -> x3, Pallas kernels: 3.97 us -> 4.42 us  [the longest x1 3.71 us: body(): pl.pallas_call(expert_kernel, out_shape=(jax.ShapeDtypeStruct((CHIPS, D),...]
  transfers between devices with their start and end apart: 2 -> 2, of which waited for: 2 -> 2; matrix products, arithmetic and copies ran while one was open for 0% -> 0% of each run, Pallas kernels for 0% -> 1%
where the time goes in v5:
time: 55.4 us; the launch traced here: 55.2 us
  blocking collectives  42.8 us (77%)
  Pallas kernels  8.35 us (15%)
  waiting for transfers between devices  2.97 us (5%)
  between operations  0.81 us (1%)
    all_to_all x1, blocking collectives, body(): own = lax.all_to_all(sent, CHIP_AXES, 0, 0, tiled=True)  24.7 us
    all_to_all x1, blocking collectives, body(): parts = lax.all_to_all(summed, CHIP_AXES, 0, 0, tiled=True)  18.1 us
    pallas_call x1, Pallas kernels, body(): pl.pallas_call(expert_kernel, out_shape=(jax.ShapeDtypeStruct((CHIPS, D),...  3.71 us
    pallas_call x1, Pallas kernels, body(): pl.pallas_call(attend_kernel, out_shape=(jax.ShapeDtypeStruct((ROWS, COLS...  3.09 us
    ppermute x2, waiting for transfers between devices, swap_cores(): return lax.ppermute(x, 'core', [(0, 1), (1, 0)])  2.97 us
  transfers between devices with their start and end apart: 2, of which 2 were waited for; matrix products, arithmetic and copies ran while one was open for 0% of the time, Pallas kernels for 1%

profile of v5, /device:TPU:0, one launch (start us, length us, event | category | flops | bytes accessed | tf_op | source)
XLA Modules:
  0.0 55.2 jit_solution(6649643313665196775)
XLA Ops:
  0.7 3.1 %attend.1 = (bf16[8,512]{1,0:T(8,128)(2,1)S(1)}, f32[8,512]{1,0:T(8,128)S(1)}) custom-call(s32[1]{0:T(128)S(6)} %copy.14.length, bf16[1,4096]{1,0:T(2,128)(2,1)} %query.1, bf16[1,4096]{1,0:T(2,128)(2,1)} %hidden_in.1, bf16[4096]{0:T(1024)(128)(2,1)} %gain.1, bf16[1,1024,512]{2,1,0:T(8,128)(2,1)} %key_latent.1, bf16[1,1024,512]{2,1,0:T(8,128)(2,1)} %value_latent.1, ...), custom_call_target="tpu_custom_call" | custom-call | tf_op jit(solution)/shard_map/attend/pallas_call | solution.py:214
  3.7 0.0 slice-start
  3.8 0.0 slice-start.2
  3.8 0.0 slice-start.4
  3.8 0.0 copy-start
  3.8 0.0 copy-start.1
  3.8 0.0 slice-start.1
  3.8 0.0 slice-start.3
  3.9 0.0 slice-start.5
  3.9 24.7 %all_to_all.10.own = bf16[64,8,512]{2,1,0:T(8,128)(2,1)S(1)} all-to-all(bf16[64,8,512]{2,1,0:T(8,128)(2,1)S(1)} %spread.1), channel_id=1, replica_groups=mesh['z'=4,'x'=4,'y'=4,'core'=2] {'x','y','z'}, dimensions={0} | all-to-all | bytes 1048576 | tf_op jit(solution)/shard_map/all_to_all | solution.py:257
  28.6 0.0 collective-permute-start
  28.6 0.0 copy-done
  28.6 0.0 copy-done.1
  28.6 0.6 %own_rows.1 = (bf16[64,4096]{1,0:T(8,128)(2,1)S(1)}, f32[64,128]{1,0:T(8,128)S(1)}) custom-call(bf16[64,8,512]{2,1,0:T(8,128)(2,1)S(1)} %all_to_all.10.own, s32[2,128]{1,0:T(2,128)S(1)} %bitcast.10, bf16[8,4096]{1,0:T(8,128)(2,1)S(1)} %bitcast.8), custom_call_target="tpu_custom_call" | custom-call | bytes 2097152 | tf_op jit(solution)/shard_map/own_rows/pallas_call | solution.py:259
  29.2 1.3 %collective-permute-done.other = bf16[64,8,512]{2,1,0:T(8,128)(2,1)S(1)} collective-permute-done((bf16[64,8,512]{2,1,0:T(8,128)(2,1)S(1)}, bf16[64,8,512]{2,1,0:T(8,128)(2,1)S(1)}, u32[]{:S(2)}, u32[]{:S(2)}) %collective-permute-start) | collective-permute-done | bytes 524320 | tf_op jit(solution)/shard_map/ppermute | solution.py:191
  30.5 0.0 slice-done
  30.5 0.0 slice-done.2
  30.5 0.0 slice-done.4
  30.5 0.0 slice-done.1
  30.5 0.0 slice-done.3
  30.5 0.0 slice-done.5
  30.5 3.7 %experts.1 = (bf16[64,4096]{1,0:T(8,128)(2,1)S(1)}, bf16[64,8,512]{2,1,0:T(8,128)(2,1)S(1)}) custom-call(bf16[64,4096]{1,0:T(8,128)(2,1)S(1)} %get-tuple-element.12.own_rows, f32[64,128]{1,0:T(8,128)S(1)} %get-tuple-element.13.own_weight, bf16[64,8,512]{2,1,0:T(8,128)(2,1)S(1)} %collective-permute-done.other, s32[2,128]{1,0:T(2,128)S(1)} %bitcast.11, ...), custom_call_target="tpu_custom_call" | custom-call | tf_op jit(solution)/shard_map/experts/pallas_call | solution.py:271
  34.3 0.2 collective-permute-start.1
  34.5 0.1 own_blocks.1.a
  34.6 1.7 %collective-permute-done.1.b = bf16[64,8,512]{2,1,0:T(8,128)(2,1)S(1)} collective-permute-done((bf16[64,8,512]{2,1,0:T(8,128)(2,1)S(1)}, bf16[64,8,512]{2,1,0:T(8,128)(2,1)S(1)}, u32[]{:S(2)}, u32[]{:S(2)}) %collective-permute-start.1) | collective-permute-done | bytes 524320 | tf_op jit(solution)/shard_map/ppermute | solution.py:191
  36.3 0.1 add_cores.1
  36.4 18.1 %all_to_all.11.parts = bf16[64,8,512]{2,1,0:T(8,128)(2,1)S(1)} all-to-all(bf16[64,8,512]{2,1,0:T(8,128)(2,1)S(1)} %add_cores.1), channel_id=1, replica_groups=mesh['z'=4,'x'=4,'y'=4,'core'=2] {'x','y','z'}, dimensions={0} | all-to-all | bytes 1048576 | tf_op jit(solution)/shard_map/all_to_all | solution.py:301
  54.5 0.7 %finish.1 = bf16[1,4096]{1,0:T(2,128)(2,1)} custom-call(bf16[64,8,512]{2,1,0:T(8,128)(2,1)S(1)} %all_to_all.11.parts, f32[8,512]{1,0:T(8,128)S(1)} %get-tuple-element.16.hidden), custom_call_target="tpu_custom_call" | custom-call | tf_op jit(solution)/shard_map/finish/pallas_call | solution.py:302
  (5 shorter events, 0.0 us)
Async XLA Ops:
  3.7 26.7 %slice-start = ((s8[7340032]{0:T(1024)(128)(4,1)}), s8[4194304]{0:T(1024)(128)(4,1)S(1)}, s32[]{:S(2)}) async-start(s8[7340032]{0:T(1024)(128)(4,1)} %bitcast.2), calls=%async_computation.2 | async-start | bytes 8388608
  3.8 26.7 %slice-start.2 = ((s8[7340032]{0:T(1024)(128)(4,1)}), s8[4194304]{0:T(1024)(128)(4,1)S(1)}, s32[]{:S(2)}) async-start(s8[7340032]{0:T(1024)(128)(4,1)} %bitcast.4), calls=%async_computation.4 | async-start | bytes 8388608
  3.8 26.7 %slice-start.4 = ((s8[7340032]{0:T(1024)(128)(4,1)}), s8[4194304]{0:T(1024)(128)(4,1)S(1)}, s32[]{:S(2)}) async-start(s8[7340032]{0:T(1024)(128)(4,1)} %bitcast.6), calls=%async_computation.6 | async-start | bytes 8388608
  3.8 24.8 %copy-start = (bf16[4096,8]{0,1:T(8,128)(2,1)S(1)}, bf16[4096,8]{0,1:T(8,128)(2,1)}, u32[]{:S(2)}) copy-start(bf16[4096,8]{0,1:T(8,128)(2,1)} %param.21) | copy-start | bytes 196612
  3.8 24.8 %copy-start.1 = (s32[128,2]{0,1:T(2,128)S(1)}, s32[128,2]{0,1:T(2,128)}, u32[]{:S(2)}) copy-start(s32[128,2]{0,1:T(2,128)} %param.22) | copy-start | bytes 3076
  3.8 26.7 %slice-start.1 = ((s8[7340032]{0:T(1024)(128)(4,1)}), s8[3145728]{0:T(1024)(128)(4,1)S(1)}, s32[]{:S(2)}) async-start(s8[7340032]{0:T(1024)(128)(4,1)} %bitcast.2), calls=%async_computation.3 | async-start | bytes 6291456
  3.8 26.7 %slice-start.3 = ((s8[7340032]{0:T(1024)(128)(4,1)}), s8[3145728]{0:T(1024)(128)(4,1)S(1)}, s32[]{:S(2)}) async-start(s8[7340032]{0:T(1024)(128)(4,1)} %bitcast.4), calls=%async_computation.5 | async-start | bytes 6291456
  3.9 26.7 %slice-start.5 = ((s8[7340032]{0:T(1024)(128)(4,1)}), s8[3145728]{0:T(1024)(128)(4,1)S(1)}, s32[]{:S(2)}) async-start(s8[7340032]{0:T(1024)(128)(4,1)} %bitcast.6), calls=%async_computation.7 | async-start | bytes 6291456
  28.6 1.9 %collective-permute-start = (bf16[64,8,512]{2,1,0:T(8,128)(2,1)S(1)}, bf16[64,8,512]{2,1,0:T(8,128)(2,1)S(1)}, u32[]{:S(2)}, u32[]{:S(2)}) collective-permute-start(bf16[64,8,512]{2,1,0:T(8,128)(2,1)S(1)} %all_to_all.10.own), channel_id=1, source_target_pairs={{0,1},{1,0},{2,3},{3,2},{4,5},{5,4},{6,7},{7,6},{8,9},{9,8},{10,11... | collective-permute-start | bytes 1572872 | tf_op jit(solution)/shard_map/ppermute | solution.py:191
  34.3 2.0 %collective-permute-start.1 = (bf16[64,8,512]{2,1,0:T(8,128)(2,1)S(1)}, bf16[64,8,512]{2,1,0:T(8,128)(2,1)S(1)}, u32[]{:S(2)}, u32[]{:S(2)}) collective-permute-start(bf16[64,8,512]{2,1,0:T(8,128)(2,1)S(1)} %get-tuple-element.15), channel_id=1, source_target_pairs={{0,1},{1,0},{2,3},{3,2},{4,5},{5,4},{6,7},{7,6},{8,9},{9,8},{10,11... | collective-permute-start | bytes 1572872 | tf_op jit(solution)/shard_map/ppermute | solution.py:191

commit v6 on v5

--- a/solution.py
+++ b/solution.py
@@ -182,7 +182,10 @@
 
 
 def finish_kernel(parts, hidden, out):
-    total = jnp.sum(parts[...].astype(F32), axis=0) + hidden[...]
+    sums = [hidden[...]] + [jnp.zeros((ROWS, COLS), F32)] * 3
+    for i in range(CHIPS):
+        sums[i % 4] = sums[i % 4] + parts[i].astype(F32)
+    total = (sums[0] + sums[1]) + (sums[2] + sums[3])
     for s in range(ROWS):
         out[0:1, s * COLS : (s + 1) * COLS] = total[s : s + 1, :].astype(BF16)
 

time: 55.4 us -> 55.4 us (level)
  no operation moved by 1% of the time
where the time goes in v6:
time: 55.4 us; the launch traced here: 55.2 us
  blocking collectives  42.8 us (77%)
  Pallas kernels  8.35 us (15%)
  waiting for transfers between devices  2.97 us (5%)
  between operations  0.81 us (1%)
    all_to_all x1, blocking collectives, body(): own = lax.all_to_all(sent, CHIP_AXES, 0, 0, tiled=True)  24.7 us
    all_to_all x1, blocking collectives, body(): parts = lax.all_to_all(summed, CHIP_AXES, 0, 0, tiled=True)  18.1 us
    pallas_call x1, Pallas kernels, body(): pl.pallas_call(expert_kernel, out_shape=(jax.ShapeDtypeStruct((CHIPS, D),...  3.71 us
    pallas_call x1, Pallas kernels, body(): pl.pallas_call(attend_kernel, out_shape=(jax.ShapeDtypeStruct((ROWS, COLS...  3.09 us
    ppermute x2, waiting for transfers between devices, swap_cores(): return lax.ppermute(x, 'core', [(0, 1), (1, 0)])  2.97 us
  transfers between devices with their start and end apart: 2, of which 2 were waited for; matrix products, arithmetic and copies ran while one was open for 0% of the time, Pallas kernels for 1%

profile of v6, /device:TPU:0, one launch (start us, length us, event | category | flops | bytes accessed | tf_op | source)
XLA Modules:
  0.0 55.2 jit_solution(5740397425996540113)
XLA Ops:
  0.7 3.1 %attend.1 = (bf16[8,512]{1,0:T(8,128)(2,1)S(1)}, f32[8,512]{1,0:T(8,128)S(1)}) custom-call(s32[1]{0:T(128)S(6)} %copy.14.length, bf16[1,4096]{1,0:T(2,128)(2,1)} %query.1, bf16[1,4096]{1,0:T(2,128)(2,1)} %hidden_in.1, bf16[4096]{0:T(1024)(128)(2,1)} %gain.1, bf16[1,1024,512]{2,1,0:T(8,128)(2,1)} %key_latent.1, bf16[1,1024,512]{2,1,0:T(8,128)(2,1)} %value_latent.1, ...), custom_call_target="tpu_custom_call" | custom-call | tf_op jit(solution)/shard_map/attend/pallas_call | solution.py:217
  3.7 0.0 slice-start
  3.8 0.0 slice-start.2
  3.8 0.0 slice-start.4
  3.8 0.0 copy-start
  3.8 0.0 copy-start.1
  3.8 0.0 slice-start.1
  3.8 0.0 slice-start.3
  3.9 0.0 slice-start.5
  3.9 24.7 %all_to_all.10.own = bf16[64,8,512]{2,1,0:T(8,128)(2,1)S(1)} all-to-all(bf16[64,8,512]{2,1,0:T(8,128)(2,1)S(1)} %spread.1), channel_id=1, replica_groups=mesh['z'=4,'x'=4,'y'=4,'core'=2] {'x','y','z'}, dimensions={0} | all-to-all | bytes 1048576 | tf_op jit(solution)/shard_map/all_to_all | solution.py:260
  28.6 0.0 collective-permute-start
  28.6 0.0 copy-done
  28.6 0.0 copy-done.1
  28.6 0.6 %own_rows.1 = (bf16[64,4096]{1,0:T(8,128)(2,1)S(1)}, f32[64,128]{1,0:T(8,128)S(1)}) custom-call(bf16[64,8,512]{2,1,0:T(8,128)(2,1)S(1)} %all_to_all.10.own, s32[2,128]{1,0:T(2,128)S(1)} %bitcast.10, bf16[8,4096]{1,0:T(8,128)(2,1)S(1)} %bitcast.8), custom_call_target="tpu_custom_call" | custom-call | bytes 2097152 | tf_op jit(solution)/shard_map/own_rows/pallas_call | solution.py:262
  29.2 1.3 %collective-permute-done.other = bf16[64,8,512]{2,1,0:T(8,128)(2,1)S(1)} collective-permute-done((bf16[64,8,512]{2,1,0:T(8,128)(2,1)S(1)}, bf16[64,8,512]{2,1,0:T(8,128)(2,1)S(1)}, u32[]{:S(2)}, u32[]{:S(2)}) %collective-permute-start) | collective-permute-done | bytes 524320 | tf_op jit(solution)/shard_map/ppermute | solution.py:194
  30.5 0.0 slice-done
  30.5 0.0 slice-done.2
  30.5 0.0 slice-done.4
  30.5 0.0 slice-done.1
  30.5 0.0 slice-done.3
  30.5 0.0 slice-done.5
  30.5 3.7 %experts.1 = (bf16[64,4096]{1,0:T(8,128)(2,1)S(1)}, bf16[64,8,512]{2,1,0:T(8,128)(2,1)S(1)}) custom-call(bf16[64,4096]{1,0:T(8,128)(2,1)S(1)} %get-tuple-element.12.own_rows, f32[64,128]{1,0:T(8,128)S(1)} %get-tuple-element.13.own_weight, bf16[64,8,512]{2,1,0:T(8,128)(2,1)S(1)} %collective-permute-done.other, s32[2,128]{1,0:T(2,128)S(1)} %bitcast.11, ...), custom_call_target="tpu_custom_call" | custom-call | tf_op jit(solution)/shard_map/experts/pallas_call | solution.py:274
  34.3 0.2 collective-permute-start.1
  34.5 0.1 own_blocks.1.a
  34.6 1.7 %collective-permute-done.1.b = bf16[64,8,512]{2,1,0:T(8,128)(2,1)S(1)} collective-permute-done((bf16[64,8,512]{2,1,0:T(8,128)(2,1)S(1)}, bf16[64,8,512]{2,1,0:T(8,128)(2,1)S(1)}, u32[]{:S(2)}, u32[]{:S(2)}) %collective-permute-start.1) | collective-permute-done | bytes 524320 | tf_op jit(solution)/shard_map/ppermute | solution.py:194
  36.3 0.1 add_cores.1
  36.4 18.1 %all_to_all.11.parts = bf16[64,8,512]{2,1,0:T(8,128)(2,1)S(1)} all-to-all(bf16[64,8,512]{2,1,0:T(8,128)(2,1)S(1)} %add_cores.1), channel_id=1, replica_groups=mesh['z'=4,'x'=4,'y'=4,'core'=2] {'x','y','z'}, dimensions={0} | all-to-all | bytes 1048576 | tf_op jit(solution)/shard_map/all_to_all | solution.py:304
  54.5 0.7 %finish.1 = bf16[1,4096]{1,0:T(2,128)(2,1)} custom-call(bf16[64,8,512]{2,1,0:T(8,128)(2,1)S(1)} %all_to_all.11.parts, f32[8,512]{1,0:T(8,128)S(1)} %get-tuple-element.16.hidden), custom_call_target="tpu_custom_call" | custom-call | tf_op jit(solution)/shard_map/finish/pallas_call | solution.py:305
  (5 shorter events, 0.0 us)
Async XLA Ops:
  3.7 26.7 %slice-start = ((s8[7340032]{0:T(1024)(128)(4,1)}), s8[4194304]{0:T(1024)(128)(4,1)S(1)}, s32[]{:S(2)}) async-start(s8[7340032]{0:T(1024)(128)(4,1)} %bitcast.2), calls=%async_computation.2 | async-start | bytes 8388608
  3.8 26.7 %slice-start.2 = ((s8[7340032]{0:T(1024)(128)(4,1)}), s8[4194304]{0:T(1024)(128)(4,1)S(1)}, s32[]{:S(2)}) async-start(s8[7340032]{0:T(1024)(128)(4,1)} %bitcast.4), calls=%async_computation.4 | async-start | bytes 8388608
  3.8 26.7 %slice-start.4 = ((s8[7340032]{0:T(1024)(128)(4,1)}), s8[4194304]{0:T(1024)(128)(4,1)S(1)}, s32[]{:S(2)}) async-start(s8[7340032]{0:T(1024)(128)(4,1)} %bitcast.6), calls=%async_computation.6 | async-start | bytes 8388608
  3.8 24.8 %copy-start = (bf16[4096,8]{0,1:T(8,128)(2,1)S(1)}, bf16[4096,8]{0,1:T(8,128)(2,1)}, u32[]{:S(2)}) copy-start(bf16[4096,8]{0,1:T(8,128)(2,1)} %param.21) | copy-start | bytes 196612
  3.8 24.8 %copy-start.1 = (s32[128,2]{0,1:T(2,128)S(1)}, s32[128,2]{0,1:T(2,128)}, u32[]{:S(2)}) copy-start(s32[128,2]{0,1:T(2,128)} %param.22) | copy-start | bytes 3076
  3.8 26.7 %slice-start.1 = ((s8[7340032]{0:T(1024)(128)(4,1)}), s8[3145728]{0:T(1024)(128)(4,1)S(1)}, s32[]{:S(2)}) async-start(s8[7340032]{0:T(1024)(128)(4,1)} %bitcast.2), calls=%async_computation.3 | async-start | bytes 6291456
  3.8 26.7 %slice-start.3 = ((s8[7340032]{0:T(1024)(128)(4,1)}), s8[3145728]{0:T(1024)(128)(4,1)S(1)}, s32[]{:S(2)}) async-start(s8[7340032]{0:T(1024)(128)(4,1)} %bitcast.4), calls=%async_computation.5 | async-start | bytes 6291456
  3.9 26.7 %slice-start.5 = ((s8[7340032]{0:T(1024)(128)(4,1)}), s8[3145728]{0:T(1024)(128)(4,1)S(1)}, s32[]{:S(2)}) async-start(s8[7340032]{0:T(1024)(128)(4,1)} %bitcast.6), calls=%async_computation.7 | async-start | bytes 6291456
  28.6 1.9 %collective-permute-start = (bf16[64,8,512]{2,1,0:T(8,128)(2,1)S(1)}, bf16[64,8,512]{2,1,0:T(8,128)(2,1)S(1)}, u32[]{:S(2)}, u32[]{:S(2)}) collective-permute-start(bf16[64,8,512]{2,1,0:T(8,128)(2,1)S(1)} %all_to_all.10.own), channel_id=1, source_target_pairs={{0,1},{1,0},{2,3},{3,2},{4,5},{5,4},{6,7},{7,6},{8,9},{9,8},{10,11... | collective-permute-start | bytes 1572872 | tf_op jit(solution)/shard_map/ppermute | solution.py:194
  34.3 2.0 %collective-permute-start.1 = (bf16[64,8,512]{2,1,0:T(8,128)(2,1)S(1)}, bf16[64,8,512]{2,1,0:T(8,128)(2,1)S(1)}, u32[]{:S(2)}, u32[]{:S(2)}) collective-permute-start(bf16[64,8,512]{2,1,0:T(8,128)(2,1)S(1)} %get-tuple-element.15), channel_id=1, source_target_pairs={{0,1},{1,0},{2,3},{3,2},{4,5},{5,4},{6,7},{7,6},{8,9},{9,8},{10,11... | collective-permute-start | bytes 1572872 | tf_op jit(solution)/shard_map/ppermute | solution.py:194
